TPU v7x, 32 devices: a whole 2x2x4 slice. The times are simulated.
32 devices in a mesh: gr: 4 (over x, core), ty: 2 (over y), tx: 4 (over z).
Axes of the slice: x: 2, y: 2, z: 4, core: 2. Of those that a mesh axis runs over, the one named last changes fastest.
Arguments:
- encoder_out: bfloat16 [32, 32, 32, 768], P('gr', 'ty', 'tx'), may hold values from -6 to 6
- code_ids: int32 [32, 32, 32], P('gr', 'ty', 'tx'), may hold values from 0 to 50264, as said below
- segments: int32 [32, 32, 32], P('gr', 'ty', 'tx'), may hold values from 0 to 2, as said below
- embed_table: bfloat16 [50272, 768], P(('ty', 'tx')), may hold values from -6 to 6
- recon_grad: bfloat16 [32, 32, 32, 768], P('gr', 'ty', 'tx'), may hold values from -6 to 6
- qkv_weight: bfloat16 [768, 2304], replicated, may hold values from -0.21875 to 0.21875
- query_bias: bfloat16 [768], replicated, may hold values from -3 to 3
- value_bias: bfloat16 [768], replicated, may hold values from -3 to 3
- out_weight: bfloat16 [768, 768], replicated, may hold values from -2.5 to 2.5
- out_bias: bfloat16 [768], replicated, may hold values from -3 to 3
- first_gain: bfloat16 [768], replicated, may hold values from 0.25 to 1.75
- first_shift: bfloat16 [768], replicated, may hold values from -1.75 to 1.75
- second_gain: bfloat16 [768], replicated, may hold values from 0.25 to 1.75
- second_shift: bfloat16 [768], replicated, may hold values from -1.75 to 1.75
- up_weight: bfloat16 [768, 3072], replicated, may hold values from -0.21875 to 0.21875
- up_bias: bfloat16 [3072], replicated, may hold values from -3 to 3
- down_weight: bfloat16 [3072, 768], replicated, may hold values from -0.109375 to 0.109375
- down_bias: bfloat16 [768], replicated, may hold values from -3 to 3
- pixel_weight: bfloat16 [768, 9, 768], replicated, may hold values from -0.078125 to 0.078125
- pixel_bias: bfloat16 [768], replicated, may hold values from -3 to 3
Outputs:
- recon: bfloat16 [32, 32, 32, 768], P('gr', 'ty', 'tx')
- input_grad: bfloat16 [32, 32, 32, 768], P('gr', 'ty', 'tx')
- qkv_weight_grad: float32 [768, 2304], P(('ty', 'tx'))
- query_bias_grad: float32 [768], P(('ty', 'tx'))
- value_bias_grad: float32 [768], P(('ty', 'tx'))
- out_weight_grad: float32 [768, 768], P(('ty', 'tx'))
- out_bias_grad: float32 [768], P(('ty', 'tx'))
- first_gain_grad: float32 [768], P(('ty', 'tx'))
- first_shift_grad: float32 [768], P(('ty', 'tx'))
- second_gain_grad: float32 [768], P(('ty', 'tx'))
- second_shift_grad: float32 [768], P(('ty', 'tx'))
- up_weight_grad: float32 [768, 3072], P(('ty', 'tx'))
- up_bias_grad: float32 [3072], P(('ty', 'tx'))
- down_weight_grad: float32 [3072, 768], P(('ty', 'tx'))
- down_bias_grad: float32 [768], P(('ty', 'tx'))
- pixel_weight_grad: float32 [768, 9, 768], P(('ty', 'tx'))
- pixel_bias_grad: float32 [768], P(('ty', 'tx'))
Inputs may be any that keep to these rules, and one draw needn't show every extreme that they name: `code_ids`: cut the stored table into 8 consecutive shares of 6284 rows, numbered as the devices of ty+tx with ty first; ids are below 50265. The ids of one device's 1024 patches fall at most 192 times into one share, and in each index of gr one share receives exactly 192 from every device. `segments`: each image is a rectangle of patches; a grid holds one to three images. Among the 8 grids of each index of gr, one is a single image.
All inputs are finite; a program needn't handle non-finite values.
Results may differ from a plain program's by a relative error of at most 0.02.
Values may be sent and summed in bfloat16 or wider, within the bound.
A program may use at most 384 MiB of HBM per device.

v0:
```python
from functools import partial

import jax
import jax.numpy as jnp
from jax import lax
from jax.sharding import PartitionSpec as P

HEADS = 12
HEAD_DIM = 64


epsilon = 1e-06
commit_weight = 0.25


def with_halo(block, sides, width):
    for axis, dim in sides:
        count = lax.axis_size(axis)
        forward = [(i, i + 1) for i in range(count - 1)]
        backward = [(target, source) for source, target in forward]
        low = lax.ppermute(
            lax.slice_in_dim(block, block.shape[dim] - width, None, axis=dim), axis, forward
        )
        high = lax.ppermute(lax.slice_in_dim(block, 0, width, axis=dim), axis, backward)
        block = jnp.concatenate([low, block, high], axis=dim)
    return block


def layer_norm(values, gain, shift):
    center = values - jnp.mean(values, axis=-1, keepdims=True)
    spread = jnp.mean(center * center, axis=-1, keepdims=True)
    return center * lax.rsqrt(spread + epsilon) * gain + shift


def exact_gelu(values):
    return jax.nn.gelu(values, approximate=False)


def matmul(left_side, right_side):
    return jnp.dot(left_side, right_side, preferred_element_type=jnp.float32)


def left_product(left_side, right_side):
    return lax.dot_general(
        left_side, right_side, (((0,), (0,)), ((), ())), preferred_element_type=jnp.float32
    )


def right_product(left_side, right_side):
    return lax.dot_general(
        left_side, right_side, (((1,), (1,)), ((), ())), preferred_element_type=jnp.float32
    )


def pad_side(array, axis_index):
    widths = [(0, 0)] * array.ndim
    widths[axis_index] = (1, 1)
    return jnp.pad(array, widths)


def blocked(array, block_size):
    return array.reshape((array.shape[0] // block_size, block_size) + array.shape[1:])


def unblock(array):
    return array.reshape((-1,) + array.shape[2:])


def head_scores(queries, key_rows, marks_query, marks_key, head_count, score_scale):
    grid_count, query_rows, features = queries.shape
    query_heads = queries.reshape(grid_count, query_rows, head_count, features // head_count)
    key_heads = key_rows.reshape(grid_count, key_rows.shape[1], head_count, features // head_count)
    scores = (
        jnp.einsum("bqhd,bkhd->bhqk", query_heads, key_heads, preferred_element_type=jnp.float32)
        * score_scale
    )
    same_image = (marks_query[:, :, None] == marks_key[:, None, :])[:, None]
    return jnp.where(same_image, scores, -1000000000.0)


def attend_block(bundle, head_count, score_scale):
    queries, key_rows, values, marks_query, marks_key = bundle
    grid_count, query_rows, features = queries.shape
    scores = head_scores(queries, key_rows, marks_query, marks_key, head_count, score_scale)
    running_max = jnp.max(scores, axis=-1, keepdims=True)
    exponent = jnp.exp(scores - running_max)
    denominator = jnp.sum(exponent, axis=-1, keepdims=True)
    probability = (exponent / denominator).astype(jnp.bfloat16)
    value_heads = values.reshape(grid_count, values.shape[1], head_count, features // head_count)
    attended = jnp.einsum(
        "bhqk,bkhd->bqhd", probability, value_heads, preferred_element_type=jnp.float32
    )
    return (
        attended.reshape(grid_count, query_rows, features).astype(jnp.bfloat16),
        running_max + jnp.log(denominator),
    )


def attend_back(bundle, head_count, score_scale):
    queries, key_rows, values, marks_query, marks_key, log_total, out_grad = bundle
    grid_count, query_rows, features = queries.shape
    head_size = features // head_count
    scores = head_scores(queries, key_rows, marks_query, marks_key, head_count, score_scale)
    probability = jnp.exp(scores - log_total)
    query_heads = queries.reshape(grid_count, query_rows, head_count, head_size)
    key_heads = key_rows.reshape(grid_count, key_rows.shape[1], head_count, head_size)
    value_heads = values.reshape(grid_count, values.shape[1], head_count, head_size)
    grad_heads = out_grad.reshape(grid_count, query_rows, head_count, head_size)
    prob_grad = jnp.einsum(
        "bqhd,bkhd->bhqk", grad_heads, value_heads, preferred_element_type=jnp.float32
    )
    inner_sum = jnp.sum(probability * prob_grad, axis=-1, keepdims=True)
    score_grad = (probability * (prob_grad - inner_sum)).astype(jnp.bfloat16)
    query_grad = (
        jnp.einsum("bhqk,bkhd->bqhd", score_grad, key_heads, preferred_element_type=jnp.float32)
        * score_scale
    )
    key_grad = (
        jnp.einsum("bhqk,bqhd->bkhd", score_grad, query_heads, preferred_element_type=jnp.float32)
        * score_scale
    )
    value_grad = jnp.einsum(
        "bhqk,bqhd->bkhd",
        probability.astype(jnp.bfloat16),
        grad_heads,
        preferred_element_type=jnp.float32,
    )
    key_count = key_rows.shape[1]
    return (
        query_grad.reshape(grid_count, query_rows, features).astype(jnp.bfloat16),
        key_grad.reshape(grid_count, key_count, features),
        value_grad.reshape(grid_count, key_count, features),
    )


def on_device(
    encoder_out,
    code_ids,
    segments,
    embed_table,
    recon_grad,
    qkv_weight,
    query_bias,
    value_bias,
    out_weight,
    out_bias,
    first_gain,
    first_shift,
    second_gain,
    second_shift,
    up_weight,
    up_bias,
    down_weight,
    down_bias,
    pixel_weight,
    pixel_bias,
):
    features = encoder_out.shape[-1]
    head_count = HEADS
    score_scale = float(HEAD_DIM) ** (-0.5)
    holder_count = lax.axis_size(("ty", "tx"))
    share_rows = embed_table.shape[0]
    flat_ids = code_ids.reshape(-1)
    row_count = flat_ids.shape[0]
    slot_count = 3 * row_count // (2 * holder_count)
    holder = flat_ids // share_rows
    offsets = flat_ids - holder * share_rows
    belongs = (holder[:, None] == jnp.arange(holder_count, dtype=jnp.int32)[None, :]).astype(
        jnp.int32
    )
    slot_rank = jnp.sum((jnp.cumsum(belongs, axis=0) - 1) * belongs, axis=1)
    slot_index = holder * slot_count + slot_rank
    requests = jnp.zeros((holder_count * slot_count,), jnp.int32).at[slot_index].set(offsets)
    requests = requests.reshape(holder_count, slot_count)
    fetched = jnp.take(
        embed_table,
        lax.all_to_all(requests, ("ty", "tx"), split_axis=0, concat_axis=0, tiled=True),
        axis=0,
    )
    returned = lax.all_to_all(fetched, ("ty", "tx"), split_axis=0, concat_axis=0, tiled=True)
    codes = returned.reshape(holder_count * slot_count, features)[slot_index].reshape(
        encoder_out.shape
    )
    marks_tile = (segments + 1).astype(jnp.bfloat16)
    arrived = (
        lax.all_to_all(encoder_out, "tx", split_axis=0, concat_axis=2, tiled=True),
        lax.all_to_all(codes, "tx", split_axis=0, concat_axis=2, tiled=True),
        lax.all_to_all(recon_grad, "tx", split_axis=0, concat_axis=2, tiled=True),
        lax.all_to_all(marks_tile, "tx", split_axis=0, concat_axis=2, tiled=True),
    )
    inputs_band, codes_band, cotangent_band, marks_band = arrived
    grid_count, band_rows, band_cols = marks_band.shape
    tokens = band_rows * band_cols
    all_rows = grid_count * tokens
    block_size = max(1, 512 // tokens)
    while grid_count % block_size:
        block_size -= 1
    start_rows = codes_band.reshape(all_rows, features).astype(jnp.float32)
    marks_query = marks_band.reshape(grid_count, tokens)
    normed, first_pull = jax.vjp(
        layer_norm, start_rows, first_gain.astype(jnp.float32), first_shift.astype(jnp.float32)
    )
    normed_low = normed.astype(jnp.bfloat16)
    projected = matmul(normed_low, qkv_weight)
    queries = (
        (projected[:, :features] + query_bias.astype(jnp.float32))
        .astype(jnp.bfloat16)
        .reshape(grid_count, tokens, features)
    )
    key_rows = (
        projected[:, features : 2 * features]
        .astype(jnp.bfloat16)
        .reshape(grid_count, tokens, features)
    )
    values = (
        (projected[:, 2 * features :] + value_bias.astype(jnp.float32))
        .astype(jnp.bfloat16)
        .reshape(grid_count, tokens, features)
    )
    bundle = (key_rows, values, marks_query)
    keys_all = lax.all_gather(bundle[0], "ty", axis=1, tiled=True)
    values_all = lax.all_gather(bundle[1], "ty", axis=1, tiled=True)
    marks_key = lax.all_gather(bundle[2], "ty", axis=1, tiled=True)
    attended_blocks, log_total = lax.map(
        partial(attend_block, head_count=head_count, score_scale=score_scale),
        (
            blocked(queries, block_size),
            blocked(keys_all, block_size),
            blocked(values_all, block_size),
            blocked(marks_query, block_size),
            blocked(marks_key, block_size),
        ),
    )
    attended = unblock(attended_blocks).reshape(all_rows, features)
    branch = matmul(attended, out_weight) + out_bias.astype(jnp.float32)
    middle = start_rows + branch
    normed_two, second_pull = jax.vjp(
        layer_norm, middle, second_gain.astype(jnp.float32), second_shift.astype(jnp.float32)
    )
    normed_two_low = normed_two.astype(jnp.bfloat16)
    hidden_pre = matmul(normed_two_low, up_weight) + up_bias.astype(jnp.float32)
    hidden_act, gelu_pull = jax.vjp(exact_gelu, hidden_pre)
    hidden_low = hidden_act.astype(jnp.bfloat16)
    output_rows = middle + (matmul(hidden_low, down_weight) + down_bias.astype(jnp.float32))
    features_low = output_rows.astype(jnp.bfloat16).reshape(
        grid_count, band_rows, band_cols, features
    )
    bundle = (features_low, marks_band, cotangent_band)
    grown = (
        with_halo(bundle[0], (("ty", 1),), 1),
        with_halo(bundle[1], (("ty", 1),), 1),
        with_halo(bundle[2], (("ty", 1),), 1),
    )
    features_pad, marks_pad, cotangent_pad = tuple((pad_side(member, 2) for member in grown))
    ahead_list = []
    behind_list = []
    for vertical in range(3):
        for lateral in range(3):
            inside = (
                marks_pad[:, vertical : vertical + band_rows, lateral : lateral + band_cols]
                == marks_band
            )
            ahead_list.append(
                jnp.where(
                    inside[..., None],
                    features_pad[:, vertical : vertical + band_rows, lateral : lateral + band_cols],
                    0,
                )
            )
            mirror_row = 2 - vertical
            mirror_col = 2 - lateral
            facing = (
                marks_pad[
                    :, mirror_row : mirror_row + band_rows, mirror_col : mirror_col + band_cols
                ]
                == marks_band
            )
            behind_list.append(
                jnp.where(
                    facing[..., None],
                    cotangent_pad[
                        :, mirror_row : mirror_row + band_rows, mirror_col : mirror_col + band_cols
                    ],
                    0,
                )
            )
    ahead = jnp.stack(ahead_list, axis=3)
    behind = jnp.stack(behind_list, axis=3)
    recon_band = jnp.einsum(
        "nhwkd,dkp->nhwp", ahead, pixel_weight, preferred_element_type=jnp.float32
    ) + pixel_bias.astype(jnp.float32)
    pixel_weight_grad = jnp.einsum(
        "nhwkd,nhwp->dkp", ahead, cotangent_band, preferred_element_type=jnp.float32
    )
    pixel_bias_grad = jnp.sum(cotangent_band.astype(jnp.float32), axis=(0, 1, 2))
    final_grad = jnp.einsum(
        "nhwkp,dkp->nhwd", behind, pixel_weight, preferred_element_type=jnp.float32
    ).reshape(all_rows, features)
    lower_grad = final_grad.astype(jnp.bfloat16)
    down_weight_grad = left_product(hidden_low, lower_grad)
    down_bias_grad = jnp.sum(lower_grad.astype(jnp.float32), axis=0)
    pre_grad = gelu_pull(right_product(lower_grad, down_weight))[0].astype(jnp.bfloat16)
    up_weight_grad = left_product(normed_two_low, pre_grad)
    up_bias_grad = jnp.sum(pre_grad.astype(jnp.float32), axis=0)
    middle_part, second_gain_grad, second_shift_grad = second_pull(
        right_product(pre_grad, up_weight)
    )
    middle_grad = final_grad + middle_part
    branch_grad = middle_grad.astype(jnp.bfloat16)
    out_weight_grad = left_product(attended, branch_grad)
    out_bias_grad = jnp.sum(branch_grad.astype(jnp.float32), axis=0)
    attended_grad = (
        right_product(branch_grad, out_weight)
        .astype(jnp.bfloat16)
        .reshape(grid_count, tokens, features)
    )
    query_blocks, key_blocks, value_blocks = lax.map(
        partial(attend_back, head_count=head_count, score_scale=score_scale),
        (
            blocked(queries, block_size),
            blocked(keys_all, block_size),
            blocked(values_all, block_size),
            blocked(marks_query, block_size),
            blocked(marks_key, block_size),
            log_total,
            blocked(attended_grad, block_size),
        ),
    )
    query_grad = unblock(query_blocks)
    bundle = (unblock(key_blocks), unblock(value_blocks))
    key_sum = lax.psum_scatter(
        bundle[0].astype(jnp.bfloat16), "ty", scatter_dimension=1, tiled=True
    )
    value_sum = lax.psum_scatter(
        bundle[1].astype(jnp.bfloat16), "ty", scatter_dimension=1, tiled=True
    )
    projected_grad = jnp.concatenate([query_grad, key_sum, value_sum], axis=-1).reshape(
        all_rows, 3 * features
    )
    qkv_weight_grad = left_product(normed_low, projected_grad)
    query_bias_grad = jnp.sum(query_grad.astype(jnp.float32), axis=(0, 1))
    value_bias_grad = jnp.sum(value_sum.astype(jnp.float32), axis=(0, 1))
    start_part, first_gain_grad, first_shift_grad = first_pull(
        right_product(projected_grad, qkv_weight)
    )
    start_grad = middle_grad + start_part
    inputs_rows = inputs_band.reshape(all_rows, features).astype(jnp.float32)
    input_band = (start_grad + 2.0 * commit_weight * (inputs_rows - start_rows)).astype(
        jnp.bfloat16
    )
    bundle = (
        recon_band.astype(jnp.bfloat16),
        input_band.reshape(grid_count, band_rows, band_cols, features),
    )
    recon_tiles = lax.all_to_all(bundle[0], "tx", split_axis=2, concat_axis=0, tiled=True)
    input_tiles = lax.all_to_all(bundle[1], "tx", split_axis=2, concat_axis=0, tiled=True)
    local_grads = (
        qkv_weight_grad,
        query_bias_grad,
        value_bias_grad,
        out_weight_grad,
        out_bias_grad,
        first_gain_grad,
        first_shift_grad,
        second_gain_grad,
        second_shift_grad,
        up_weight_grad,
        up_bias_grad,
        down_weight_grad,
        down_bias_grad,
        pixel_weight_grad,
        pixel_bias_grad,
    )
    tile_shares = (
        lax.psum_scatter(
            local_grads[0].astype(jnp.bfloat16), ("ty", "tx"), scatter_dimension=0, tiled=True
        ).astype(jnp.float32),
        lax.psum_scatter(
            local_grads[1].astype(jnp.bfloat16), ("ty", "tx"), scatter_dimension=0, tiled=True
        ).astype(jnp.float32),
        lax.psum_scatter(
            local_grads[2].astype(jnp.bfloat16), ("ty", "tx"), scatter_dimension=0, tiled=True
        ).astype(jnp.float32),
        lax.psum_scatter(
            local_grads[3].astype(jnp.bfloat16), ("ty", "tx"), scatter_dimension=0, tiled=True
        ).astype(jnp.float32),
        lax.psum_scatter(
            local_grads[4].astype(jnp.bfloat16), ("ty", "tx"), scatter_dimension=0, tiled=True
        ).astype(jnp.float32),
        lax.psum_scatter(
            local_grads[5].astype(jnp.bfloat16), ("ty", "tx"), scatter_dimension=0, tiled=True
        ).astype(jnp.float32),
        lax.psum_scatter(
            local_grads[6].astype(jnp.bfloat16), ("ty", "tx"), scatter_dimension=0, tiled=True
        ).astype(jnp.float32),
        lax.psum_scatter(
            local_grads[7].astype(jnp.bfloat16), ("ty", "tx"), scatter_dimension=0, tiled=True
        ).astype(jnp.float32),
        lax.psum_scatter(
            local_grads[8].astype(jnp.bfloat16), ("ty", "tx"), scatter_dimension=0, tiled=True
        ).astype(jnp.float32),
        lax.psum_scatter(
            local_grads[9].astype(jnp.bfloat16), ("ty", "tx"), scatter_dimension=0, tiled=True
        ).astype(jnp.float32),
        lax.psum_scatter(
            local_grads[10].astype(jnp.bfloat16), ("ty", "tx"), scatter_dimension=0, tiled=True
        ).astype(jnp.float32),
        lax.psum_scatter(
            local_grads[11].astype(jnp.bfloat16), ("ty", "tx"), scatter_dimension=0, tiled=True
        ).astype(jnp.float32),
        lax.psum_scatter(
            local_grads[12].astype(jnp.bfloat16), ("ty", "tx"), scatter_dimension=0, tiled=True
        ).astype(jnp.float32),
        lax.psum_scatter(
            local_grads[13].astype(jnp.bfloat16), ("ty", "tx"), scatter_dimension=0, tiled=True
        ).astype(jnp.float32),
        lax.psum_scatter(
            local_grads[14].astype(jnp.bfloat16), ("ty", "tx"), scatter_dimension=0, tiled=True
        ).astype(jnp.float32),
    )
    summed = (
        lax.psum(tile_shares[0].astype(jnp.bfloat16), "gr").astype(jnp.float32),
        lax.psum(tile_shares[1].astype(jnp.bfloat16), "gr").astype(jnp.float32),
        lax.psum(tile_shares[2].astype(jnp.bfloat16), "gr").astype(jnp.float32),
        lax.psum(tile_shares[3].astype(jnp.bfloat16), "gr").astype(jnp.float32),
        lax.psum(tile_shares[4].astype(jnp.bfloat16), "gr").astype(jnp.float32),
        lax.psum(tile_shares[5].astype(jnp.bfloat16), "gr").astype(jnp.float32),
        lax.psum(tile_shares[6].astype(jnp.bfloat16), "gr").astype(jnp.float32),
        lax.psum(tile_shares[7].astype(jnp.bfloat16), "gr").astype(jnp.float32),
        lax.psum(tile_shares[8].astype(jnp.bfloat16), "gr").astype(jnp.float32),
        lax.psum(tile_shares[9].astype(jnp.bfloat16), "gr").astype(jnp.float32),
        lax.psum(tile_shares[10].astype(jnp.bfloat16), "gr").astype(jnp.float32),
        lax.psum(tile_shares[11].astype(jnp.bfloat16), "gr").astype(jnp.float32),
        lax.psum(tile_shares[12].astype(jnp.bfloat16), "gr").astype(jnp.float32),
        lax.psum(tile_shares[13].astype(jnp.bfloat16), "gr").astype(jnp.float32),
        lax.psum(tile_shares[14].astype(jnp.bfloat16), "gr").astype(jnp.float32),
    )
    return (
        recon_tiles,
        input_tiles,
        summed[0],
        summed[1],
        summed[2],
        summed[3],
        summed[4],
        summed[5],
        summed[6],
        summed[7],
        summed[8],
        summed[9],
        summed[10],
        summed[11],
        summed[12],
        summed[13],
        summed[14],
    )


def solution(mesh):
    in_specs = (
        P("gr", "ty", "tx", None),
        P("gr", "ty", "tx"),
        P("gr", "ty", "tx"),
        P(("ty", "tx"), None),
        P("gr", "ty", "tx", None),
        P(),
        P(),
        P(),
        P(),
        P(),
        P(),
        P(),
        P(),
        P(),
        P(),
        P(),
        P(),
        P(),
        P(),
        P(),
    )
    out_specs = (
        P("gr", "ty", "tx", None),
        P("gr", "ty", "tx", None),
        P(("ty", "tx"), None),
        P(("ty", "tx")),
        P(("ty", "tx")),
        P(("ty", "tx"), None),
        P(("ty", "tx")),
        P(("ty", "tx")),
        P(("ty", "tx")),
        P(("ty", "tx")),
        P(("ty", "tx")),
        P(("ty", "tx"), None),
        P(("ty", "tx")),
        P(("ty", "tx"), None),
        P(("ty", "tx")),
        P(("ty", "tx"), None, None),
        P(("ty", "tx")),
    )
    return jax.shard_map(
        on_device, mesh=mesh, in_specs=in_specs, out_specs=out_specs, check_vma=False
    )
```

profile of v0, /device:TPU:0, one launch (start us, length us, event | category | flops | bytes accessed | tf_op | source)
XLA Modules:
  0.0 1485.5 jit_solution(11487479264674776304)
XLA Ops:
  53.3 11.7 gather_fusion
  68.4 58.3 %all_to_all.113 = bf16[8,192,768]{2,1,0:T(8,128)(2,1)} all-to-all(bf16[8,192,768]{2,1,0:T(8,128)(2,1)} %broadcast_select_fusion), channel_id=1, replica_groups=mesh['gr'=4,'ty'=2,'tx'=4] {'ty','tx'}, dimensions={0} | all-to-all | bytes 4718592 | tf_op jit(solution)/shard_map/all_to_all | solution.py:180
  138.6 27.9 %all-to-all-done.5 = bf16[8,16,8,768]{3,2,1,0:T(8,128)(2,1)} async-done(((bf16[8,16,8,768]{3,2,1,0:T(8,128)(2,1)}), bf16[8,16,8,768]{3,2,1,0:T(8,128)(2,1)}, u32[]{:S(2)}, u32[]{:S(2)}) %all-to-all-start.5) | async-done | bytes 1572896 | tf_op jit(solution)/shard_map/all_to_all | solution.py:188
  262.2 15.3 %fusion.22 = f32[2,16,32,768,1]{3,2,1,0,4:T(8,128)S(1)} fusion(bf16[2,16,32,9,768]{4,2,1,0,3:T(8,128)(2,1)} %copy-done.31, bf16[768,9,768]{2,0,1:T(8,128)(2,1)} %param.42), kind=kOutput, calls=%fused_computation.63 | convolution fusion | flops 10871635968 | bytes 27918336 | tf_op jit(solution)/shard_map/nhwkp,dkp->nhwd/dot_general | solution.py:296
  290.5 46.5 %all-gather.3.cloned.1.call-done = bf16[2,1024,768]{1,2,0:T(8,128)(2,1)} async-done(((bf16[2,512,768]{1,2,0:T(8,128)(2,1)}), bf16[2,1024,768]{1,2,0:T(8,128)(2,1)}) %all-gather.3.cloned.1.call-update) | async-done | bytes 3145744 | tf_op jit(solution)/shard_map/all_gather | solution.py:222
  337.0 91.2 %while.26 = (s32[]{:T(128)}, bf16[2,1,512,768]{3,2,0,1:T(8,128)(2,1)}, f32[2,1,12,512,1]{3,2,4,1,0:T(8,128)}, bf16[2,1,1024,768]{2,3,1,0:T(8,128)(2,1)}, bf16[2,...) while((s32[]{:T(128)}, ...), condition=%wide.region_9.10_spmd, body=%wide.region_6.9_spmd.sunk | while | flops 1687021568 | bytes 194610384 | solution.py:224
  341.9 10.6 fusion.172
  352.6 12.3 fusion.173
  387.5 10.6 fusion.172
  398.2 12.3 fusion.173
  433.3 35.8 %multiply_convert_fusion.2 = (bf16[1024,3072]{1,0:T(8,128)(2,1)}, f32[1024,3072]{1,0:T(8,128)}, f32[1024,3072]{1,0:T(8,128)}) fusion(f32[3072]{0:T(1024)S(1)} %copy-done.73, bf16[768,3072]{1,0:T(8,128)(2,1)S(1)} %bitcast.410, f32[1024,768]{1,0:T(8,128)S(1)} %get-tuple-element.287, f32[768]{0:T(1024)S(1)} %copy-done.75, f32[768]{0:T(1024)S(1)} %copy-done.64, ...), kind=kOutput, calls=%fused_computation.48 | convolution fusion | flops 5043388416 | bytes 39348224 | tf_op jit(solution)/shard_map/dot_general | solution.py:40
  469.1 17.2 %fusion.112 = (bf16[3072]{0:T(1024)(128)(2,1)}, bf16[1024,3072]{1,0:T(8,128)(2,1)}) fusion(f32[1024,3072]{1,0:T(8,128)} %get-tuple-element.256, bf16[1024,768]{1,0:T(8,128)(2,1)} %bitcast_convert_fusion.1, bf16[3072,768]{1,0:T(8,128)(2,1)} %param.40, f32[1024,3072]{1,0:T(8,128)} %get-tuple-element.288, f32[3072]{0:T(1024)} %convert_element_type.333), kind=kOutput, calls=%fused_computation.244 | convolution fusion | flops 4882166784 | bytes 37767168 | tf_op jit(solution)/shard_map/dot_general | solution.py:50
  502.7 210.3 %while.27 = (s32[]{:T(128)}, bf16[2,1,512,768]{2,3,1,0:T(8,128)(2,1)}, bf16[2,1,1024,768]{3,2,0,1:T(8,128)(2,1)}, bf16[2,1,1024,768]{3,2,0,1:T(8,128)(2,1)}, bf1...) while((s32[]{:T(128)}, ...), condition=%wide.region_16.17_spmd, body=%wide.region_14.16_spmd.sunk | while | flops 4123781120 | bytes 264783248 | solution.py:317
  515.4 10.1 fusion.185
  525.5 12.7 fusion.187
  540.8 18.8 %multiply_reduce_fusion.8 = (f32[12,512]{1,0:T(8,128)}, f32[12,512,1024]{2,1,0:T(8,128)}) fusion(f32[12,512,1024]{2,1,0:T(8,128)} %fusion.185, f32[12,512]{1,0:T(8,128)} %dynamic-slice_bitcast_fusion.2, pred[512,1024]{1,0:T(8,128)(4,1)} %broadcast_compare_fusion.5, bf16[512,12,64]{0,2,1:T(8,128)(2,1)} %bitcast.365, bf16[1024,12,64]{0,2,1:T(8,128)(2,1)} %bitcast.358), kind=kOutput, calls=%fused_computation.21.clone.1 | convolution fusion | flops 836757504 | bytes 53264384 | tf_op jit(solution)/shard_map/while/body/eval_jaxpr/bqhd,bkhd->bhqk/dot_general | solution.py:109
  559.7 22.2 %multiply_convert_fusion.5 = bf16[12,512,1024]{2,1,0:T(8,128)(2,1)} fusion(f32[12,512,1024]{2,1,0:T(8,128)} %get-tuple-element.421, f32[12,512,1024]{2,1,0:T(8,128)} %fusion.185, f32[12,512]{1,0:T(8,128)} %get-tuple-element.422, f32[12,512]{1,0:T(8,128)} %dynamic-slice_bitcast_fusion.2, pred[512,1024]{1,0:T(8,128)(4,1)} %broadcast_compare_fusion.5), kind=kLoop, calls=%fused_computation.20.clone.1 | loop fusion | flops 37748736 | bytes 63488000 | tf_op jit(solution)/shard_map/while/body/eval_jaxpr/convert_element_type | solution.py:113
  630.5 12.7 fusion.187
  645.8 18.8 %multiply_reduce_fusion.8 = (f32[12,512]{1,0:T(8,128)}, f32[12,512,1024]{2,1,0:T(8,128)}) fusion(f32[12,512,1024]{2,1,0:T(8,128)} %fusion.185, f32[12,512]{1,0:T(8,128)} %dynamic-slice_bitcast_fusion.2, pred[512,1024]{1,0:T(8,128)(4,1)} %broadcast_compare_fusion.5, bf16[512,12,64]{0,2,1:T(8,128)(2,1)} %bitcast.365, bf16[1024,12,64]{0,2,1:T(8,128)(2,1)} %bitcast.358), kind=kOutput, calls=%fused_computation.21.clone.1 | convolution fusion | flops 836757504 | bytes 53264384 | tf_op jit(solution)/shard_map/while/body/eval_jaxpr/bqhd,bkhd->bhqk/dot_general | solution.py:109
  664.7 22.2 %multiply_convert_fusion.5 = bf16[12,512,1024]{2,1,0:T(8,128)(2,1)} fusion(f32[12,512,1024]{2,1,0:T(8,128)} %get-tuple-element.421, f32[12,512,1024]{2,1,0:T(8,128)} %fusion.185, f32[12,512]{1,0:T(8,128)} %get-tuple-element.422, f32[12,512]{1,0:T(8,128)} %dynamic-slice_bitcast_fusion.2, pred[512,1024]{1,0:T(8,128)(4,1)} %broadcast_compare_fusion.5), kind=kLoop, calls=%fused_computation.20.clone.1 | loop fusion | flops 37748736 | bytes 63488000 | tf_op jit(solution)/shard_map/while/body/eval_jaxpr/convert_element_type | solution.py:113
  718.0 10.3 convolution_convert_fusion
  729.0 10.5 convolution_convert_fusion.1
  778.9 23.4 %reduce-scatter.10.cloned.1.call-done = bf16[2,512,768]{2,1,0:T(8,128)(2,1)} async-done(((bf16[2,1024,768]{2,1,0:T(8,128)(2,1)}), bf16[2,512,768]{2,1,0:T(8,128)(2,1)}) %reduce-scatter.10.cloned.1.call-update) | async-done | bytes 1572880 | tf_op jit(solution)/shard_map/reduce_scatter | solution.py:334
  811.0 17.5 %fusion.21 = bf16[768,9,768]{2,0,1:T(8,128)(2,1)} fusion(bf16[2,16,32,9,768]{4,2,3,1,0:T(8,128)(2,1)} %fusion.61, bf16[2,16,32,768,1]{3,2,1,0,4:T(8,128)(2,1)} %bitcast.371), kind=kOutput, calls=%fused_computation.62 | convolution fusion | flops 10876944384 | bytes 26345472 | tf_op jit(solution)/shard_map/nhwkd,nhwp->dkp/dot_general | solution.py:292
  833.2 40.6 %all-to-all-done.6 = bf16[8,16,8,768]{3,2,1,0:T(8,128)(2,1)} async-done(((bf16[8,16,8,768]{3,2,1,0:T(8,128)(2,1)}), bf16[8,16,8,768]{3,2,1,0:T(8,128)(2,1)}, u32[]{:S(2)}, u32[]{:S(2)}) %all-to-all-start.6) | async-done | bytes 1572896 | tf_op jit(solution)/shard_map/all_to_all | solution.py:186
  877.1 17.4 %fusion.34 = bf16[2,16,32,768]{3,2,1,0:T(8,128)(2,1)S(1)} fusion(bf16[2,16,32,9,768]{4,2,3,1,0:T(8,128)(2,1)} %fusion.61, bf16[768,9,768]{2,0,1:T(8,128)(2,1)} %param.42, f32[768]{0:T(1024)S(1)} %convert_element_type.337), kind=kOutput, calls=%fused_computation.89 | convolution fusion | flops 10873208832 | bytes 26348544 | tf_op jit(solution)/shard_map/nhwkd,dkp->nhwp/dot_general | solution.py:289
  916.7 45.1 %all-to-all-done.4 = bf16[2,16,32,768]{3,1,0,2:T(8,128)(2,1)} async-done(((bf16[2,16,32,768]{3,1,0,2:T(8,128)(2,1)}), bf16[2,16,32,768]{3,1,0,2:T(8,128)(2,1)}, u32[]{:S(2)}, u32[]{:S(2)}) %all-to-all-start.4) | async-done | bytes 1572896 | tf_op jit(solution)/shard_map/all_to_all | solution.py:355
  966.3 56.4 %reduce-scatter.18.cloned.1.call-done = bf16[384,768]{1,0:T(8,128)(2,1)} async-done(((bf16[3072,768]{1,0:T(8,128)(2,1)}), bf16[384,768]{1,0:T(8,128)(2,1)}) %reduce-scatter.18.cloned.1.call-update) | async-done | bytes 589840 | tf_op jit(solution)/shard_map/reduce_scatter | solution.py:408
  1022.6 98.9 %reduce-scatter.16.cloned.1.call-done = bf16[96,3072]{1,0:T(8,128)(2,1)} async-done(((bf16[768,3072]{1,0:T(8,128)(2,1)}), bf16[96,3072]{1,0:T(8,128)(2,1)}) %reduce-scatter.16.cloned.1.call-update) | async-done | bytes 589840 | tf_op jit(solution)/shard_map/reduce_scatter | solution.py:402
  1121.5 82.6 %reduce-scatter.12.cloned.1.call-done = bf16[96,2304]{1,0:T(8,128)(2,1)} async-done(((bf16[768,2304]{1,0:T(8,128)(2,1)}), bf16[96,2304]{1,0:T(8,128)(2,1)}) %reduce-scatter.12.cloned.1.call-update) | async-done | bytes 442384 | tf_op jit(solution)/shard_map/reduce_scatter | solution.py:375
  1204.1 183.1 %reduce-scatter.20.cloned.1.call-done = bf16[96,9,768]{2,0,1:T(8,128)(2,1)} async-done(((bf16[768,9,768]{2,0,1:T(8,128)(2,1)}), bf16[96,9,768]{2,0,1:T(8,128)(2,1)}) %reduce-scatter.20.cloned.1.call-update) | async-done | bytes 1327120 | tf_op jit(solution)/shard_map/reduce_scatter | solution.py:414
  1400.7 36.3 %all-reduce.13 = (bf16[768]{0:T(1024)(128)(2,1)}, bf16[768]{0:T(1024)(128)(2,1)}, bf16[768]{0:T(1024)(128)(2,1)}, bf16[768]{0:T(1024)(128)(2,1)}, bf16[768]{0:T(...) all-reduce(bf16[768]{0:T(1024)(128)(2,1)S(1)} %reduce_sum.251, ...), channel_id=5, replica_groups=mesh['gr'=4,'ty'=2,'tx'=4] {'ty','tx'}, use_global_device_ids=true, to_apply=%region_24.25.clone | all-reduce | flops 9984 | bytes 39936
  (460 shorter events, 469.8 us)
Async XLA Ops:
  7.2 223.7 %copy-start = (bf16[768,2304]{1,0:T(8,128)(2,1)S(1)}, bf16[768,2304]{1,0:T(8,128)(2,1)}, u32[]{:S(2)}) copy-start(bf16[768,2304]{1,0:T(8,128)(2,1)} %param.29) | copy-start | bytes 10616836
  34.3 13.8 all-to-all-start.1
  48.1 20.3 %all-to-all-start = ((bf16[4,2,128]{2,1,0:T(2,128)(2,1)}), bf16[4,2,128]{2,1,0:T(2,128)(2,1)}, u32[]{:S(2)}, u32[]{:S(2)}) async-start(bf16[4,2,128]{2,1,0:T(2,128)(2,1)} %reshape.684), calls=%async_computation | async-start | bytes 4096 | tf_op jit(solution)/shard_map/all_to_all | solution.py:189
  68.4 62.7 %copy-start.72 = (s32[1024,1]{0,1:T(1,128)S(1)}, s32[1024,1]{0,1:T(1,128)}, u32[]{:S(2)}) copy-start(s32[1024,1]{0,1:T(1,128)} %copy-done.71) | copy-start | bytes 12292
  126.7 39.9 %all-to-all-start.5 = ((bf16[8,16,8,768]{3,2,1,0:T(8,128)(2,1)}), bf16[8,16,8,768]{3,2,1,0:T(8,128)(2,1)}, u32[]{:S(2)}, u32[]{:S(2)}) async-start(bf16[8,16,8,768]{3,2,1,0:T(8,128)(2,1)} %param.28), calls=%async_computation.5 | async-start | bytes 3145728 | tf_op jit(solution)/shard_map/all_to_all | solution.py:188
  166.6 50.1 %all-to-all-start.3 = ((bf16[8,16,8,768]{3,2,1,0:T(8,128)(2,1)}), bf16[8,16,8,768]{3,2,1,0:T(8,128)(2,1)}, u32[]{:S(2)}, u32[]{:S(2)}) async-start(bf16[8,16,8,768]{3,2,1,0:T(8,128)(2,1)} %bitcast.386), calls=%async_computation.3 | async-start | bytes 3145728 | tf_op jit(solution)/shard_map/all_to_all | solution.py:187
  170.9 119.5 %all-gather.5.cloned.1.call-start = ((), (), s32[]{:S(2)}) async-start(), calls=%async_computation.16 | async-start | bytes 4718592 | tf_op jit(solution)/shard_map/all_gather | solution.py:221
  184.4 9.5 collective-permute-start
  186.9 7.0 collective-permute-start.1
  210.7 31.6 %collective-permute-start.4 = (bf16[2,1,32,768]{3,2,1,0:T(8,128)(2,1)}, bf16[2,1,32,768]{3,2,1,0:T(8,128)(2,1)}, u32[]{:S(2)}, u32[]{:S(2)}) collective-permute-start(bf16[2,1,32,768]{3,2,1,0:T(8,128)(2,1)} %get-tuple-element.269), channel_id=1, source_target_pairs={{0,4},{1,5},{2,6},{3,7},{8,12},{9,13},{10,14},{11,15},{16,20},{17,... | collective-permute-start | bytes 294920 | tf_op jit(solution)/shard_map/ppermute | solution.py:21
  215.2 27.1 %collective-permute-start.5 = (bf16[2,1,32,768]{3,2,1,0:T(8,128)(2,1)}, bf16[2,1,32,768]{3,2,1,0:T(8,128)(2,1)}, u32[]{:S(2)}, u32[]{:S(2)}) collective-permute-start(bf16[2,1,32,768]{3,2,1,0:T(8,128)(2,1)} %get-tuple-element.270), channel_id=1, source_target_pairs={{4,0},{5,1},{6,2},{7,3},{12,8},{13,9},{14,10},{15,11},{20,16},{21,... | collective-permute-start | bytes 294920 | tf_op jit(solution)/shard_map/ppermute | solution.py:24
  242.3 94.7 %all-gather.3.cloned.1.call-start = ((), (), s32[]{:S(2)}) async-start(), calls=%async_computation.15 | async-start | bytes 4718592 | tf_op jit(solution)/shard_map/all_gather | solution.py:222
  261.9 517.0 %reduce-scatter.8.cloned.1.call-start = ((), (), s32[]{:S(2)}) async-start(), calls=%async_computation.17 | async-start | bytes 4718592 | tf_op jit(solution)/shard_map/reduce_scatter | solution.py:331
  279.2 57.8 %copy-start.30 = (bf16[2,1,1024]{2,1,0:T(2,128)(2,1)S(1)}, bf16[2,1,1024]{2,1,0:T(2,128)(2,1)}, u32[]{:S(2)}) copy-start(bf16[2,1,1024]{2,1,0:T(2,128)(2,1)} %copy.118) | copy-start | bytes 12292
  279.2 57.8 %copy-start.32 = (bf16[2,1,512]{2,1,0:T(2,128)(2,1)S(1)}, bf16[2,1,512]{2,1,0:T(2,128)(2,1)}, u32[]{:S(2)}) copy-start(bf16[2,1,512]{2,1,0:T(2,128)(2,1)} %reshape_reshape.18) | copy-start | bytes 6148
  337.0 91.2 %copy-start.77 = (f32[768]{0:T(1024)S(1)}, f32[768]{0:T(1024)}, u32[]{:S(2)}) copy-start(f32[768]{0:T(1024)} %convert_element_type.329) | copy-start | bytes 9220
  432.6 63.6 %copy-start.21 = (f32[1024,768]{1,0:T(8,128)}, f32[1024,768]{1,0:T(8,128)S(1)}, u32[]{:S(2)}) copy-start(f32[1024,768]{1,0:T(8,128)S(1)} %get-tuple-element.287) | copy-start | bytes 9437188
  432.6 63.5 %copy-start.61 = (f32[1024]{0:T(1024)}, f32[1024]{0:T(1024)S(1)}, u32[]{:S(2)}) copy-start(f32[1024]{0:T(1024)S(1)} %broadcast_multiply_fusion.1) | copy-start | bytes 12292
  433.3 62.8 %copy-start.66 = (f32[1024]{0:T(1024)}, f32[1024]{0:T(1024)S(1)}, u32[]{:S(2)}) copy-start(f32[1024]{0:T(1024)S(1)} %fusion.99) | copy-start | bytes 12292
  713.0 89.4 %reduce-scatter.10.cloned.1.call-start = ((), (), s32[]{:S(2)}) async-start(), calls=%async_computation.18 | async-start | bytes 4718592 | tf_op jit(solution)/shard_map/reduce_scatter | solution.py:334
  713.6 252.7 %reduce-scatter.14.cloned.1.call-start = ((), (), s32[]{:S(2)}) async-start(), calls=%async_computation.20 | async-start | bytes 1327104 | tf_op jit(solution)/shard_map/reduce_scatter | solution.py:384
  718.0 304.6 %reduce-scatter.18.cloned.1.call-start = ((), (), s32[]{:S(2)}) async-start(), calls=%async_computation.22 | async-start | bytes 5308416 | tf_op jit(solution)/shard_map/reduce_scatter | solution.py:408
  728.3 393.2 %reduce-scatter.16.cloned.1.call-start = ((), (), s32[]{:S(2)}) async-start(), calls=%async_computation.21 | async-start | bytes 5308416 | tf_op jit(solution)/shard_map/reduce_scatter | solution.py:402
  739.5 464.6 %reduce-scatter.12.cloned.1.call-start = ((), (), s32[]{:S(2)}) async-start(), calls=%async_computation.19 | async-start | bytes 3981312 | tf_op jit(solution)/shard_map/reduce_scatter | solution.py:375
  751.0 6.2 collective-permute-start.2
  752.9 6.8 collective-permute-start.3
  810.9 576.2 %reduce-scatter.20.cloned.1.call-start = ((), (), s32[]{:S(2)}) async-start(), calls=%async_computation.23 | async-start | bytes 11943936 | tf_op jit(solution)/shard_map/reduce_scatter | solution.py:414
  828.5 45.2 %all-to-all-start.6 = ((bf16[8,16,8,768]{3,2,1,0:T(8,128)(2,1)}), bf16[8,16,8,768]{3,2,1,0:T(8,128)(2,1)}, u32[]{:S(2)}, u32[]{:S(2)}) async-start(bf16[8,16,8,768]{3,2,1,0:T(8,128)(2,1)} %param.24), calls=%async_computation.8 | async-start | bytes 3145728 | tf_op jit(solution)/shard_map/all_to_all | solution.py:186
  896.5 65.3 %all-to-all-start.4 = ((bf16[2,16,32,768]{3,1,0,2:T(8,128)(2,1)}), bf16[2,16,32,768]{3,1,0,2:T(8,128)(2,1)}, u32[]{:S(2)}, u32[]{:S(2)}) async-start(bf16[2,16,32,768]{3,1,0,2:T(8,128)(2,1)} %copy.137), calls=%async_computation.4 | async-start | bytes 3145728 | tf_op jit(solution)/shard_map/all_to_all | solution.py:355
  916.7 470.5 %copy-start.83 = (u32[32]{0:T(128)S(1)}, u32[32]{0:T(128)}, u32[]{:S(2)}) copy-start(u32[32]{0:T(128)} %constant.189) | copy-start | bytes 388
  961.8 504.4 %all-to-all-start.7 = ((bf16[2,16,32,768]{3,1,0,2:T(8,128)(2,1)}), bf16[2,16,32,768]{3,1,0,2:T(8,128)(2,1)}, u32[]{:S(2)}, u32[]{:S(2)}) async-start(bf16[2,16,32,768]{3,1,0,2:T(8,128)(2,1)} %copy.150), calls=%async_computation.9 | async-start | bytes 3145728 | tf_op jit(solution)/shard_map/all_to_all | solution.py:356
  966.2 503.4 %all-reduce.18.cloned.1.call-start = ((), (), s32[]{:S(2)}) async-start(), calls=%async_computation.24 | async-start | bytes 6193152 | tf_op jit(solution)/shard_map/psum | solution.py:422
  (91 other events, 663.5 us)
Sparse Core Ops, SparseCore 0:
  242.4 48.0 all-gather.4
  292.0 44.9 all-gather.2
  713.1 43.3 reduce-scatter.7
  758.7 43.6 reduce-scatter.9
  806.2 72.3 reduce-scatter.13
  882.1 140.4 reduce-scatter.17
  1026.3 95.1 reduce-scatter.15
  1125.1 78.9 reduce-scatter.11
  1207.7 179.4 reduce-scatter.19
  1390.0 67.9 all-reduce.17
where the time goes:
time: 1500 us; the launch traced here: 1490 us
  waiting for transfers between devices  619 us (41%)
  matrix products  334 us (22%)
  local copies, waits for them, and re-layouts  185 us (12%)
  other arithmetic  177 us (12%)
  blocking collectives  107 us (7%)
  starting transfers between devices  46.9 us (3%)
  between operations  16.8 us (1%)
    reduce_scatter x1, waiting for transfers between devices, on_device(): lax.psum_scatter(local_grads[13].astype(jnp.bfloat16), ('ty', 'tx'), scat...  183 us
    reduce_scatter x1, waiting for transfers between devices, on_device(): lax.psum_scatter(local_grads[9].astype(jnp.bfloat16), ('ty', 'tx'), scatt...  98.9 us
    reduce_scatter x1, waiting for transfers between devices, on_device(): lax.psum_scatter(local_grads[0].astype(jnp.bfloat16), ('ty', 'tx'), scatt...  82.6 us
    all_to_all x1, blocking collectives, on_device(): lax.all_to_all(fetched, ('ty', 'tx'), split_axis=0, concat_axis=0, tiled=...  58.3 us
    reduce_scatter x1, waiting for transfers between devices, on_device(): lax.psum_scatter(local_grads[11].astype(jnp.bfloat16), ('ty', 'tx'), scat...  56.4 us
    dot_general x4, matrix products, matmul(): return jnp.dot(left_side, right_side, preferred_element_type=jnp.float32)  53 us
    all_gather x1, waiting for transfers between devices, on_device(): values_all = lax.all_gather(bundle[1], 'ty', axis=1, tiled=True)  46.5 us
    all_to_all x1, waiting for transfers between devices, on_device(): lax.all_to_all(bundle[0], 'tx', split_axis=2, concat_axis=0, tiled=True)  45.1 us
  transfers between devices with their start and end apart: 23, of which 12 were waited for; matrix products, arithmetic and copies ran while one was open for 18% of the time, Pallas kernels for 0%

commit v1 on v0

--- a/solution.py
+++ b/solution.py
@@ -3,6 +3,8 @@
 import jax
 import jax.numpy as jnp
 from jax import lax
+from jax.experimental import pallas as pl
+from jax.experimental.pallas import tpu as pltpu
 from jax.sharding import PartitionSpec as P
 
 HEADS = 12
@@ -133,7 +135,7 @@
     )
 
 
-def on_device(
+def on_device_bands(
     encoder_out,
     code_ids,
     segments,
@@ -456,6 +458,367 @@
     )
 
 
+far = float(2.0**30)
+
+
+def nt(left_side, right_side):
+    return lax.dot_general(
+        left_side, right_side, (((1,), (1,)), ((), ())), preferred_element_type=jnp.float32
+    )
+
+
+def nn(left_side, right_side):
+    return lax.dot_general(
+        left_side, right_side, (((1,), (0,)), ((), ())), preferred_element_type=jnp.float32
+    )
+
+
+def mark_columns(marks):
+    lane = lax.broadcasted_iota(jnp.int32, (1, 128), 1) % 64
+    hot = marks[:, None] == lane
+    query_side = jnp.where(hot, 1.0, 0.0)
+    key_side = jnp.where((lane < 3) & ~hot, -far, 0.0)
+    return query_side.astype(jnp.bfloat16), key_side.astype(jnp.bfloat16)
+
+
+def attend_kernel(q_ref, k_ref, v_ref, qa_ref, ka_ref, o_ref, col_ref):
+    lane = lax.broadcasted_iota(jnp.int32, (1, 128), 1)
+    low = lane < 64
+    local = lane % 64
+    one = jnp.ones((), jnp.bfloat16)
+    queries, key_rows, values = q_ref[...], k_ref[...], v_ref[...]
+    query_marks, key_marks = qa_ref[...], ka_ref[...]
+    outs = []
+    logs = []
+    for head in range(2):
+        own = low if head == 0 else ~low
+        scores = nt(jnp.where(own, queries, query_marks), jnp.where(own, key_rows, key_marks))
+        top = jnp.max(scores, axis=1, keepdims=True)
+        weights = jnp.exp(scores - top).astype(jnp.bfloat16)
+        sums = nn(weights, jnp.where(own, values, one))
+        outs.append(sums / pltpu.roll(sums, 64, 1))
+        logs.append(top + jnp.log(sums))
+    o_ref[...] = jnp.where(low, outs[0], outs[1]).astype(jnp.bfloat16)
+    minus = -jnp.where(low, logs[1], logs[0])
+    first = minus.astype(jnp.bfloat16).astype(jnp.float32)
+    second = (minus - first).astype(jnp.bfloat16).astype(jnp.float32)
+    third = minus - first - second
+    columns = jnp.where(
+        local == 3,
+        first,
+        jnp.where(local == 4, second, jnp.where(local == 5, third, query_marks.astype(jnp.float32))),
+    )
+    col_ref[...] = columns.astype(jnp.bfloat16)
+
+
+def attend(queries, key_rows, values, query_marks, key_marks):
+    tokens, features = queries.shape
+    pair = pl.BlockSpec((tokens, 128), lambda i: (0, i))
+    shared = pl.BlockSpec((tokens, 128), lambda i: (0, 0))
+    shape = jax.ShapeDtypeStruct((tokens, features), jnp.bfloat16)
+    return pl.pallas_call(
+        attend_kernel,
+        grid=(features // 128,),
+        in_specs=[pair, pair, pair, shared, shared],
+        out_specs=[pair, pair],
+        out_shape=[shape, shape],
+        compiler_params=pltpu.CompilerParams(vmem_limit_bytes=48 * 2**20),
+        cost_estimate=pl.CostEstimate(
+            flops=16 * tokens * tokens * features,
+            bytes_accessed=10 * tokens * features,
+            transcendentals=tokens * tokens * features // 64,
+        ),
+        name="attend",
+    )(queries, key_rows, values, query_marks, key_marks)
+
+
+def attend_back_kernel(
+    q_ref, k_ref, v_ref, col_ref, ka_ref, o_ref, g_ref, dq_ref, dk_ref, dv_ref, k_sum, v_sum, *, step
+):
+    lane = lax.broadcasted_iota(jnp.int32, (1, 128), 1)
+    low = lane < 64
+    local = lane % 64
+    zero = jnp.zeros((), jnp.bfloat16)
+    one = jnp.ones((), jnp.bfloat16)
+    key_rows, values = k_ref[...], v_ref[...]
+    tokens = key_rows.shape[0]
+    key_columns = jnp.where((local >= 3) & (local < 6), one, ka_ref[...])
+    value_columns = jnp.where(local < 2, one, zero)
+    keys_of = [jnp.where(low, key_rows, key_columns), jnp.where(low, key_columns, key_rows)]
+    values_of = [jnp.where(low, values, value_columns), jnp.where(low, value_columns, values)]
+    keys_across = key_rows.T
+    upper = lax.broadcasted_iota(jnp.int32, (128, 1), 0) < 64
+    k_sum[...] = jnp.zeros_like(k_sum)
+    v_sum[...] = jnp.zeros_like(v_sum)
+
+    def one_block(i, _):
+        rows = pl.ds(pl.multiple_of(i * step, step), step)
+        queries, columns = q_ref[rows, :], col_ref[rows, :]
+        grad, out = g_ref[rows, :], o_ref[rows, :]
+        both = grad.astype(jnp.float32) * out.astype(jnp.float32)
+        of_low = -jnp.sum(jnp.where(low, both, 0.0), axis=1, keepdims=True)
+        of_high = -jnp.sum(jnp.where(low, 0.0, both), axis=1, keepdims=True)
+        inner = jnp.where(low, of_high, of_low)
+        first = inner.astype(jnp.bfloat16).astype(jnp.float32)
+        grad_columns = jnp.where(
+            local == 0, first, jnp.where(local == 1, inner - first, 0.0)
+        ).astype(jnp.bfloat16)
+        query_parts, key_parts, value_parts = [], [], []
+        for head in range(2):
+            own = low if head == 0 else ~low
+            weights = jnp.exp(nt(keys_of[head], jnp.where(own, queries, columns)))
+            change = nt(values_of[head], jnp.where(own, grad, grad_columns))
+            score_grad = (weights * change).astype(jnp.bfloat16)
+            value_parts.append(nn(weights.astype(jnp.bfloat16), grad))
+            key_parts.append(nn(score_grad, queries))
+            query_parts.append(nn(keys_across, score_grad))
+        k_sum[...] += jnp.where(low, key_parts[0], key_parts[1])
+        v_sum[...] += jnp.where(low, value_parts[0], value_parts[1])
+        query_grad = jnp.where(upper, query_parts[0], query_parts[1]).T
+        dq_ref[rows, :] = (query_grad * HEAD_DIM**-0.5).astype(jnp.bfloat16)
+        return 0
+
+    lax.fori_loop(0, tokens // step, one_block, 0)
+    dk_ref[...] = k_sum[...].astype(jnp.bfloat16)
+    dv_ref[...] = v_sum[...].astype(jnp.bfloat16)
+
+
+def attend_back_grid(queries, key_rows, values, columns, key_marks, out, grad):
+    tokens, features = queries.shape
+    pair = pl.BlockSpec((tokens, 128), lambda i: (0, i))
+    shared = pl.BlockSpec((tokens, 128), lambda i: (0, 0))
+    shape = jax.ShapeDtypeStruct((tokens, features), jnp.bfloat16)
+    return pl.pallas_call(
+        partial(attend_back_kernel, step=min(512, tokens)),
+        grid=(features // 128,),
+        in_specs=[pair, pair, pair, pair, shared, pair, pair],
+        out_specs=[pair, pair, pair],
+        out_shape=[shape, shape, shape],
+        scratch_shapes=[pltpu.VMEM((tokens, 128), jnp.float32)] * 2,
+        compiler_params=pltpu.CompilerParams(vmem_limit_bytes=48 * 2**20),
+        cost_estimate=pl.CostEstimate(
+            flops=24 * tokens * tokens * features,
+            bytes_accessed=18 * tokens * features,
+            transcendentals=tokens * tokens * features // 64,
+        ),
+        name="attend_back",
+    )(queries, key_rows, values, columns, key_marks, out, grad)
+
+
+def fetch_codes(code_ids, embed_table):
+    features = embed_table.shape[1]
+    holder_count = lax.axis_size(("ty", "tx"))
+    share_rows = embed_table.shape[0]
+    flat_ids = code_ids.reshape(-1)
+    row_count = flat_ids.shape[0]
+    slot_count = 3 * row_count // (2 * holder_count)
+    starts = jnp.arange(1, holder_count, dtype=jnp.int32) * share_rows
+    holder = jnp.sum((flat_ids[:, None] >= starts[None, :]).astype(jnp.int32), axis=1)
+    offsets = flat_ids - holder * share_rows
+    belongs = holder[:, None] == jnp.arange(holder_count, dtype=jnp.int32)[None, :]
+    place = jnp.arange(row_count, dtype=jnp.int32)
+    before = (place[:, None] > place[None, :]).astype(jnp.bfloat16)
+    ranks = matmul(before, belongs.astype(jnp.bfloat16))
+    slot_rank = jnp.sum(jnp.where(belongs, ranks, 0.0), axis=1).astype(jnp.int32)
+    slot_index = holder * slot_count + slot_rank
+    requests = jnp.zeros((holder_count * slot_count,), jnp.int32)
+    requests = requests.at[slot_index].set(offsets, mode="promise_in_bounds", unique_indices=True)
+    requests = requests.reshape(holder_count, slot_count)
+    asked = lax.all_to_all(requests, ("ty", "tx"), split_axis=0, concat_axis=0, tiled=True)
+    fetched = embed_table.at[asked.reshape(-1)].get(mode="promise_in_bounds")
+    fetched = fetched.reshape(holder_count, slot_count, features)
+    returned = lax.all_to_all(fetched, ("ty", "tx"), split_axis=0, concat_axis=0, tiled=True)
+    returned = returned.reshape(holder_count * slot_count, features)
+    return returned.at[slot_index].get(mode="promise_in_bounds")
+
+
+def to_grid(tiles):
+    down, across = lax.axis_size("ty"), lax.axis_size("tx")
+    parts = lax.all_to_all(tiles, ("ty", "tx"), split_axis=0, concat_axis=0, tiled=True)
+    parts = parts.reshape((down, across) + tiles.shape[1:])
+    parts = jnp.moveaxis(parts, 1, 2)
+    return parts.reshape((down * tiles.shape[1], across * tiles.shape[2]) + tiles.shape[3:])
+
+
+def to_tiles(grid):
+    down, across = lax.axis_size("ty"), lax.axis_size("tx")
+    rows, cols = grid.shape[0] // down, grid.shape[1] // across
+    parts = grid.reshape((down, rows, across, cols) + grid.shape[2:])
+    parts = jnp.moveaxis(parts, 2, 1).reshape((down * across, rows, cols) + grid.shape[2:])
+    return lax.all_to_all(parts, ("ty", "tx"), split_axis=0, concat_axis=0, tiled=True)
+
+
+def neighbours(rows_grid, marks_grid, direction):
+    height, width = marks_grid.shape
+    padded = jnp.pad(rows_grid, ((1, 1), (1, 1), (0, 0)))
+    marks_pad = jnp.pad(marks_grid, ((1, 1), (1, 1)), constant_values=-1)
+    taps = []
+    for vertical in range(3):
+        for lateral in range(3):
+            down = vertical if direction > 0 else 2 - vertical
+            right = lateral if direction > 0 else 2 - lateral
+            inside = marks_pad[down : down + height, right : right + width] == marks_grid
+            rows = padded[down : down + height, right : right + width]
+            taps.append(jnp.where(inside[..., None], rows, 0).reshape(height * width, -1))
+    return jnp.concatenate(taps, axis=1)
+
+
+def gelu_parts(values):
+    spread = jnp.exp(-0.5 * values * values)
+    upto = 0.5 * (1.0 + lax.erf(values * 0.7071067811865476))
+    return values * upto, upto + values * spread * 0.3989422804014327
+
+
+def sum_shares(grad):
+    shares = lax.psum_scatter(
+        grad.astype(jnp.bfloat16), ("ty", "tx", "gr"), scatter_dimension=0, tiled=True
+    )
+    return lax.all_gather(shares, "gr", axis=0, tiled=True).astype(jnp.float32)
+
+
+def on_device_grids(
+    encoder_out,
+    code_ids,
+    segments,
+    embed_table,
+    recon_grad,
+    qkv_weight,
+    query_bias,
+    value_bias,
+    out_weight,
+    out_bias,
+    first_gain,
+    first_shift,
+    second_gain,
+    second_shift,
+    up_weight,
+    up_bias,
+    down_weight,
+    down_bias,
+    pixel_weight,
+    pixel_bias,
+):
+    features = encoder_out.shape[-1]
+    wide = jnp.float32
+    marks_grid = to_grid(segments)
+    cotangent_grid = to_grid(recon_grad)
+    height, width = marks_grid.shape
+    tokens = height * width
+    codes_tile = fetch_codes(code_ids, embed_table).reshape(encoder_out.shape)
+    start_rows = to_grid(codes_tile).reshape(tokens, features).astype(wide)
+    query_marks, key_marks = mark_columns(marks_grid.reshape(tokens))
+
+    cotangent = cotangent_grid.reshape(tokens, features)
+    behind = neighbours(cotangent_grid, marks_grid, -1)
+    pixel_flat = pixel_weight.reshape(features, 9 * features)
+    final_grad = right_product(behind, pixel_flat)
+    lower_grad = final_grad.astype(jnp.bfloat16)
+    pixel_bias_grad = jnp.sum(cotangent.astype(wide), axis=0)
+    down_bias_grad = jnp.sum(lower_grad.astype(wide), axis=0)
+    hidden_grad = right_product(lower_grad, down_weight)
+
+    normed, first_pull = jax.vjp(
+        layer_norm, start_rows, first_gain.astype(wide), first_shift.astype(wide)
+    )
+    normed_low = normed.astype(jnp.bfloat16)
+    projected = matmul(normed_low, qkv_weight)
+    scale = HEAD_DIM**-0.5
+    queries = (projected[:, :features] + query_bias.astype(wide)).astype(jnp.bfloat16)
+    queries = queries * jnp.asarray(scale, jnp.bfloat16)
+    key_rows = projected[:, features : 2 * features].astype(jnp.bfloat16)
+    values = (projected[:, 2 * features :] + value_bias.astype(wide)).astype(jnp.bfloat16)
+    attended, columns = attend(queries, key_rows, values, query_marks, key_marks)
+    middle = start_rows + (matmul(attended, out_weight) + out_bias.astype(wide))
+    normed_two, second_pull = jax.vjp(
+        layer_norm, middle, second_gain.astype(wide), second_shift.astype(wide)
+    )
+    normed_two_low = normed_two.astype(jnp.bfloat16)
+    hidden_pre = matmul(normed_two_low, up_weight) + up_bias.astype(wide)
+    hidden_act, slope = gelu_parts(hidden_pre)
+    hidden_low = hidden_act.astype(jnp.bfloat16)
+    pre_grad = (hidden_grad * slope).astype(jnp.bfloat16)
+    output_rows = middle + (matmul(hidden_low, down_weight) + down_bias.astype(wide))
+    features_low = output_rows.astype(jnp.bfloat16)
+
+    pixel_weight_grad = left_product(features_low, behind)
+    down_weight_grad = left_product(hidden_low, lower_grad)
+    up_weight_grad = left_product(normed_two_low, pre_grad)
+    up_bias_grad = jnp.sum(pre_grad.astype(wide), axis=0)
+
+    ahead = neighbours(features_low.reshape(height, width, features), marks_grid, 1)
+    pixel_rows = jnp.swapaxes(pixel_weight, 0, 1).reshape(9 * features, features)
+    recon_grid = (matmul(ahead, pixel_rows) + pixel_bias.astype(wide)).astype(jnp.bfloat16)
+    recon_tiles = to_tiles(recon_grid.reshape(height, width, features))
+
+    middle_part, second_gain_grad, second_shift_grad = second_pull(
+        right_product(pre_grad, up_weight)
+    )
+    middle_grad = final_grad + middle_part
+    branch_grad = middle_grad.astype(jnp.bfloat16)
+    out_weight_grad = left_product(attended, branch_grad)
+    out_bias_grad = jnp.sum(branch_grad.astype(wide), axis=0)
+    attended_grad = right_product(branch_grad, out_weight).astype(jnp.bfloat16)
+    query_grad, key_grad, value_grad = attend_back_grid(
+        queries, key_rows, values, columns, key_marks, attended, attended_grad
+    )
+    projected_grad = jnp.concatenate([query_grad, key_grad, value_grad], axis=1)
+    qkv_weight_grad = left_product(normed_low, projected_grad)
+    query_bias_grad = jnp.sum(query_grad.astype(wide), axis=0)
+    value_bias_grad = jnp.sum(value_grad.astype(wide), axis=0)
+    start_part, first_gain_grad, first_shift_grad = first_pull(
+        right_product(projected_grad, qkv_weight)
+    )
+    start_grad = middle_grad + start_part
+    share = (start_grad - 2.0 * commit_weight * start_rows).astype(jnp.bfloat16)
+    share_tiles = to_tiles(share.reshape(height, width, features))
+    input_tiles = (
+        share_tiles.astype(wide) + 2.0 * commit_weight * encoder_out.astype(wide)
+    ).astype(jnp.bfloat16)
+
+    vectors = [
+        query_bias_grad,
+        value_bias_grad,
+        out_bias_grad,
+        first_gain_grad,
+        first_shift_grad,
+        second_gain_grad,
+        second_shift_grad,
+        up_bias_grad,
+        down_bias_grad,
+        pixel_bias_grad,
+    ]
+    shards = lax.axis_size(("ty", "tx"))
+    packed = jnp.concatenate([v.reshape(shards, -1) for v in vectors], axis=1).reshape(-1)
+    packed = sum_shares(packed)
+    sums = []
+    at = 0
+    for vector in vectors:
+        size = vector.shape[0] // shards
+        sums.append(packed[at : at + size])
+        at += size
+    (query_bias_sum, value_bias_sum, out_bias_sum, first_gain_sum, first_shift_sum) = sums[:5]
+    (second_gain_sum, second_shift_sum, up_bias_sum, down_bias_sum, pixel_bias_sum) = sums[5:]
+    return (
+        recon_tiles,
+        input_tiles,
+        sum_shares(qkv_weight_grad),
+        query_bias_sum,
+        value_bias_sum,
+        sum_shares(out_weight_grad),
+        out_bias_sum,
+        first_gain_sum,
+        first_shift_sum,
+        second_gain_sum,
+        second_shift_sum,
+        sum_shares(up_weight_grad),
+        up_bias_sum,
+        sum_shares(down_weight_grad),
+        down_bias_sum,
+        sum_shares(pixel_weight_grad).reshape(-1, 9, features),
+        pixel_bias_sum,
+    )
+
+
 def solution(mesh):
     in_specs = (
         P("gr", "ty", "tx", None),
@@ -498,6 +861,12 @@
         P(("ty", "tx"), None, None),
         P(("ty", "tx")),
     )
+    def on_device(encoder_out, *rest):
+        members = mesh.shape["ty"] * mesh.shape["tx"]
+        whole_grids = encoder_out.shape[0] == members
+        body = on_device_grids if whole_grids else on_device_bands
+        return body(encoder_out, *rest)
+
     return jax.shard_map(
         on_device, mesh=mesh, in_specs=in_specs, out_specs=out_specs, check_vma=False
     )

time: 1500 us -> 925 us (0.62)
  waiting for transfers between devices: 619 us -> 342 us
  matrix products: 334 us -> 135 us
  other arithmetic: 177 us -> 62.4 us
  Pallas kernels: 0 us -> 61 us
  local copies, waits for them, and re-layouts: 185 us -> 133 us
  blocking collectives: 107 us -> 136 us
  starting transfers between devices: 46.9 us -> 31.1 us
    dot_general x17 -> x0, matrix products: 209 us -> none  [the longest x4 41.5 us: head_scores(): jnp.einsum('bqhd,bkhd->bhqk', query_heads, key_heads, preferred_element_t...]
    reduce_scatter x7 -> x5, waiting for transfers between devices: 444 us -> 274 us  [sum_shares(): lax.psum_scatter(grad.astype(jnp.bfloat16), ('ty', 'tx', 'gr'), scatter_d...]
    pallas_call x0 -> x2, Pallas kernels: none -> 61 us  [the longest x1 37.2 us: attend_back_grid(): pl.pallas_call(partial(attend_back_kernel, step=min(512, tokens)), grid=(...]
    all_to_all x7 -> x6, waiting for transfers between devices: 117 us -> 58.1 us  [the longest x3 28.8 us: to_grid(): lax.all_to_all(tiles, ('ty', 'tx'), split_axis=0, concat_axis=0, tiled=True)]
    convert_element_type x33 -> x20, other arithmetic: 81.6 us -> 25.3 us  [the longest x4 3.91 us: sum_shares(): return lax.all_gather(shares, 'gr', axis=0, tiled=True).astype(jnp.float32)]
    all_gather x2 -> x1, waiting for transfers between devices: 53.9 us -> 10 us  [sum_shares(): return lax.all_gather(shares, 'gr', axis=0, tiled=True).astype(jnp.float32)]
    unnamed x170 -> x190, local copies, waits for them, and re-layouts: 32.9 us -> 67 us
    dynamic_update_slice x12 -> x0, local copies, waits for them, and re-layouts: 30.7 us -> none  [the longest x6 17.8 us: on_device(): lax.map(partial(attend_back, head_count=head_count, score_scale=score_sca...]
  transfers between devices with their start and end apart: 23 -> 12, of which waited for: 12 -> 7; matrix products, arithmetic and copies ran while one was open for 18% -> 26% of each run, Pallas kernels for 0% -> 4%
where the time goes in v1:
time: 925 us; the launch traced here: 918 us
  waiting for transfers between devices  342 us (37%)
  blocking collectives  136 us (15%)
  matrix products  135 us (15%)
  local copies, waits for them, and re-layouts  133 us (14%)
  other arithmetic  62.4 us (7%)
  Pallas kernels  61 us (7%)
  starting transfers between devices  31.1 us (3%)
  between operations  16.7 us (2%)
    reduce_scatter x5, waiting for transfers between devices, sum_shares(): lax.psum_scatter(grad.astype(jnp.bfloat16), ('ty', 'tx', 'gr'), scatter_d...  274 us
    unnamed x190, local copies, waits for them, and re-layouts  67 us
    all_to_all x1, blocking collectives, fetch_codes(): lax.all_to_all(fetched, ('ty', 'tx'), split_axis=0, concat_axis=0, tiled=...  59.1 us
    dot_general x5, matrix products, right_product(): lax.dot_general(left_side, right_side, (((1,), (1,)), ((), ())), preferre...  51.2 us
    unnamed x2, blocking collectives  48.7 us
    dot_general x5, matrix products, left_product(): lax.dot_general(left_side, right_side, (((0,), (0,)), ((), ())), preferre...  43.9 us
    dot_general x6, matrix products, matmul(): return jnp.dot(left_side, right_side, preferred_element_type=jnp.float32)  39.8 us
    pallas_call x1, Pallas kernels, attend_back_grid(): pl.pallas_call(partial(attend_back_kernel, step=min(512, tokens)), grid=(...  37.2 us
  transfers between devices with their start and end apart: 12, of which 7 were waited for; matrix products, arithmetic and copies ran while one was open for 26% of the time, Pallas kernels for 4%

profile of v1, /device:TPU:0, one launch (start us, length us, event | category | flops | bytes accessed | tf_op | source)
XLA Modules:
  0.0 917.6 jit_solution(3316191588744509787)
XLA Ops:
  15.4 7.3 all-to-all-start.1
  33.2 11.7 %gather_fusion = bf16[1536,768]{1,0:T(8,128)(2,1)} fusion(bf16[6284,768]{1,0:T(8,128)(2,1)} %param.23, s32[2048]{0:T(1024)S(1)} %pad_clamp_fusion), kind=kCustom, calls=%fused_computation | custom fusion | bytes 4724736 | tf_op jit(solution)/shard_map/gather | solution.py:628
  44.9 59.1 %all_to_all.39 = bf16[8,192,768]{2,1,0:T(8,128)(2,1)} all-to-all(bf16[8,192,768]{2,1,0:T(8,128)(2,1)} %bitcast.107), channel_id=1, replica_groups=mesh['gr'=4,'ty'=2,'tx'=4] {'ty','tx'}, dimensions={0} | all-to-all | bytes 4718592 | tf_op jit(solution)/shard_map/all_to_all | solution.py:630
  108.4 7.5 gather_fusion.1
  115.9 28.8 %all-to-all-done.5 = bf16[8,16,8,768]{3,2,1,0:T(8,128)(2,1)} async-done(((bf16[8,16,8,768]{3,2,1,0:T(8,128)(2,1)}), bf16[8,16,8,768]{3,2,1,0:T(8,128)(2,1)}, u32[]{:S(2)}, u32[]{:S(2)}) %all-to-all-start.5) | async-done | bytes 1572896 | tf_op jit(solution)/shard_map/all_to_all | solution.py:637
  180.5 5.3 fusion.27
  216.5 23.9 %attend.1 = (bf16[1024,768]{1,0:T(8,128)(2,1)S(1)}, bf16[1024,768]{1,0:T(8,128)(2,1)S(1)}) custom-call(bf16[1024,768]{1,0:T(8,128)(2,1)S(1)} %get-tuple-element.141.q_ref, bf16[1024,768]{1,0:T(8,128)(2,1)} %get-tuple-element.140.k_ref, bf16[1024,768]{1,0:T(8,128)(2,1)} %fusion.7.v_ref, bf16[1024,128]{1,0:T(8,128)(2,1)S(1)} %copy-done.9, ...), custom_call_target="tpu_custom_call" | custom-call | flops 12884901888 | bytes 7864320 | tf_op jit(solution)/shard_map/attend/pallas_call | solution.py:519
  245.2 9.4 %multiply_convert_fusion = (bf16[1024,3072]{1,0:T(8,128)(2,1)S(1)}, f32[1024,3072]{1,0:T(8,128)}) fusion(f32[3072]{0:T(1024)S(1)} %copy-done.59, bf16[768,3072]{1,0:T(8,128)(2,1)S(1)} %bitcast.140, f32[1024,768]{1,0:T(8,128)S(1)} %get-tuple-element.185, f32[768]{0:T(1024)S(1)} %copy-done.64, f32[768]{0:T(1024)S(1)} %copy-done.54, f32[1024]{0:T(1024)S(1)} %fusion.47, ...), kind=kOutput, calls=%fused_computation.10 | convolution fusion | flops 4854644736 | bytes 26765312 | tf_op jit(solution)/shard_map/dot_general | solution.py:42
  263.4 18.6 %convolution_convert_fusion = bf16[768,6912]{1,0:T(8,128)(2,1)} fusion(bf16[1024,768]{1,0:T(8,128)(2,1)S(1)} %add_convert_fusion.2, bf16[1024,6912]{1,0:T(8,128)(2,1)} %constant_dynamic-update-slice_fusion.9), kind=kOutput, calls=%fused_computation.12 | convolution fusion | flops 10876944384 | bytes 26345472 | tf_op jit(solution)/shard_map/dot_general | solution.py:46
  282.1 15.7 %copy.136 = bf16[768,9,768]{0,2,1:T(8,128)(2,1)} copy(bf16[768,9,768]{2,0,1:T(8,128)(2,1)} %param.38) | data formatting | bytes 21233664 | tf_op args[18]
  297.8 15.6 %fusion.62 = f32[1024,768]{1,0:T(8,128)S(1)} fusion(bf16[1024,6912]{1,0:T(8,128)(2,1)} %constant_dynamic-update-slice_fusion.9, bf16[768,6912]{0,1:T(8,128)(2,1)} %bitcast.106), kind=kOutput, calls=%fused_computation.163 | convolution fusion | flops 10871635968 | bytes 27918336 | tf_op jit(solution)/shard_map/dot_general | solution.py:52
  313.4 14.0 %fusion.60 = (bf16[3072]{0:T(1024)(128)(2,1)}, bf16[1024,3072]{1,0:T(8,128)(2,1)S(1)}) fusion(f32[1024,3072]{1,0:T(8,128)} %get-tuple-element.187, f32[3072]{0:T(1024)S(1)} %copy-done.60, bf16[3072,768]{1,0:T(8,128)(2,1)} %param.36, f32[1024,768]{1,0:T(8,128)S(1)} %fusion.62), kind=kOutput, calls=%fused_computation.161 | convolution fusion | flops 4870370304 | bytes 26757120 | tf_op jit(solution)/shard_map/dot_general | solution.py:52
  327.4 10.9 %multiply_reduce_fusion = (bf16[768]{0:T(1024)(128)(2,1)}, f32[1024]{0:T(1024)S(1)}, bf16[768]{0:T(1024)(128)(2,1)}, f32[1024,768]{1,0:T(8,128)S(1)}) fusion(f32[1024,768]{1,0:T(8,128)S(1)} %copy-done.18, f32[1024]{0:T(1024)S(1)} %fusion.47, f32[1024]{0:T(1024)S(1)} %broadcast_multiply_fusion.1, f32[768]{0:T(1024)S(1)} %copy-done.54, ...), kind=kOutput, calls=%fused_computation.31 | convolution fusion | flops 4838126592 | bytes 17319936 | tf_op jit(solution)/shard_map/dot_general | solution.py:52
  348.4 37.2 %attend_back.1 = (bf16[1024,768]{1,0:T(8,128)(2,1)S(1)}, bf16[1024,768]{1,0:T(8,128)(2,1)S(1)}, bf16[1024,768]{1,0:T(8,128)(2,1)S(1)}) custom-call(bf16[1024,768]{1,0:T(8,128)(2,1)} %copy-done.1, bf16[1024,768]{1,0:T(8,128)(2,1)} %get-tuple-element.140.k_ref, bf16[1024,768]{1,0:T(8,128)(2,1)} %fusion.7.v_ref, bf16[1024,768]{1,0:T(8,128)(2,1)} %copy-done.12, ...), custom_call_target="tpu_custom_call" | custom-call | flops 19327352832 | bytes 14155776 | tf_op jit(solution)/shard_map/attend_back/pallas_call | solution.py:591
  394.9 5.3 convolution_convert_fusion.3
  400.9 10.4 %convolution_convert_fusion.2 = bf16[768,3072]{1,0:T(8,128)(2,1)} fusion(bf16[1024,3072]{1,0:T(8,128)(2,1)} %copy-done.73, f32[1024,768]{1,0:T(8,128)} %copy-done.17, f32[768]{0:T(1024)S(1)} %copy-done.65, f32[768]{0:T(1024)S(1)} %copy-done.54, f32[1024]{0:T(1024)S(1)} %fusion.47, f32[1024]{0:T(1024)S(1)} %broadcast_multiply_fusion.1), kind=kOutput, calls=%fused_computation.14 | convolution fusion | flops 4838129664 | bytes 14170112 | tf_op jit(solution)/shard_map/dot_general | solution.py:46
  412.9 12.5 %fusion.19 = (bf16[32,32,768]{2,1,0:T(8,128)(2,1)}, bf16[32,32,768]{2,1,0:T(8,128)(2,1)S(1)}, bf16[32,32,768]{2,1,0:T(8,128)(2,1)S(1)}, bf16[32,32,768]{2,1,0:T(...) fusion(bf16[32,32,768]{2,1,0:T(8,128)(2,1)} %bitcast.108, ...), kind=kLoop, calls=%fused_computation.68 | loop fusion | flops 6291456 | bytes 14163968 | tf_op jit(solution)/shard_map/jit(_where)/select_n | solution.py:662
  432.3 7.1 convolution_convert_fusion.1
  446.3 17.2 %add_convert_fusion.1 = bf16[1024,768]{1,0:T(8,128)(2,1)S(1)} fusion(bf16[1024,6912]{1,0:T(8,128)(2,1)} %constant_dynamic-update-slice_fusion, bf16[6912,768]{1,0:T(8,128)(2,1)} %bitcast.105, f32[768]{0:T(1024)S(1)} %copy-done.68), kind=kOutput, calls=%fused_computation.37 | convolution fusion | flops 10873208832 | bytes 26348544 | tf_op jit(solution)/shard_map/dot_general | solution.py:42
  464.8 6.1 all-to-all-start.4
  470.9 8.2 fusion.51
  485.0 24.2 %all-to-all-done.4 = bf16[8,16,8,768]{3,2,1,0:T(8,128)(2,1)} async-done(((bf16[8,16,8,768]{3,2,1,0:T(8,128)(2,1)}), bf16[8,16,8,768]{3,2,1,0:T(8,128)(2,1)}, u32[]{:S(2)}, u32[]{:S(2)}) %all-to-all-start.4) | async-done | bytes 1572896 | tf_op jit(solution)/shard_map/all_to_all | solution.py:648
  530.8 42.9 %all-reduce.4 = bf16[9984]{0:T(1024)(128)(2,1)} all-reduce(bf16[9984]{0:T(1024)(128)(2,1)} %convert_element_type.234), channel_id=3, replica_groups=mesh['gr'=4,'ty'=2,'tx'=4] {'ty','tx','gr'}, use_global_device_ids=true, to_apply=%region_22.23.clone | all-reduce | flops 9984 | bytes 39936
  574.7 5.8 all-reduce.3
  581.8 6.0 all_gather.20
  592.1 66.7 %reduce-scatter.6.cloned.1.call-done = bf16[24,2304]{1,0:T(8,128)(2,1)} async-done(((bf16[768,2304]{1,0:T(8,128)(2,1)}), bf16[24,2304]{1,0:T(8,128)(2,1)}) %reduce-scatter.6.cloned.1.call-update) | async-done | bytes 110608 | tf_op jit(solution)/shard_map/reduce_scatter | solution.py:673
  658.8 6.8 all_gather.18
  666.5 103.5 %reduce-scatter.10.cloned.1.call-done = bf16[24,3072]{1,0:T(8,128)(2,1)} async-done(((bf16[768,3072]{1,0:T(8,128)(2,1)}), bf16[24,3072]{1,0:T(8,128)(2,1)}) %reduce-scatter.10.cloned.1.call-update) | async-done | bytes 147472 | tf_op jit(solution)/shard_map/reduce_scatter | solution.py:673
  770.0 7.7 all_gather.21
  778.8 103.6 %reduce-scatter.12.cloned.1.call-done = bf16[96,768]{1,0:T(8,128)(2,1)} async-done(((bf16[3072,768]{1,0:T(8,128)(2,1)}), bf16[96,768]{1,0:T(8,128)(2,1)}) %reduce-scatter.12.cloned.1.call-update) | async-done | bytes 147472 | tf_op jit(solution)/shard_map/reduce_scatter | solution.py:673
  882.4 7.7 all_gather.22
  891.1 10.0 %all-gather.2.cloned.1.call-done = bf16[96,6912]{1,0:T(8,128)(2,1)} async-done(((bf16[24,6912]{1,0:T(8,128)(2,1)}), bf16[96,6912]{1,0:T(8,128)(2,1)}) %all-gather.2.cloned.1.call-update) | async-done | bytes 1327120 | tf_op jit(solution)/shard_map/all_gather | solution.py:676
  (313 shorter events, 184.5 us)
Async XLA Ops:
  7.2 202.5 %copy-start = (bf16[768,2304]{1,0:T(8,128)(2,1)S(1)}, bf16[768,2304]{1,0:T(8,128)(2,1)}, u32[]{:S(2)}) copy-start(bf16[768,2304]{1,0:T(8,128)(2,1)} %param.25) | copy-start | bytes 10616836
  15.4 13.8 %all-to-all-start.1 = ((s32[8,1,192]{2,1,0:T(1,128)}), s32[8,1,192]{2,1,0:T(1,128)S(1)}, u32[]{:S(2)}, u32[]{:S(2)}) async-start(s32[8,1,192]{2,1,0:T(1,128)} %all_to_all.25), calls=%async_computation.1 | async-start | bytes 16384 | tf_op jit(solution)/shard_map/all_to_all | solution.py:627
  29.2 15.7 %all-to-all-start = ((s32[8,1,128]{2,1,0:T(1,128)}), s32[8,1,128]{2,1,0:T(1,128)}, u32[]{:S(2)}, u32[]{:S(2)}) async-start(s32[8,1,128]{2,1,0:T(1,128)} %reshape.456), calls=%async_computation | async-start | bytes 8192 | tf_op jit(solution)/shard_map/all_to_all | solution.py:637
  44.9 63.4 %copy-start.57 = (s32[1024,1]{0,1:T(1,128)S(1)}, s32[1024,1]{0,1:T(1,128)}, u32[]{:S(2)}) copy-start(s32[1024,1]{0,1:T(1,128)} %copy-done.56) | copy-start | bytes 12292
  104.1 40.6 %all-to-all-start.5 = ((bf16[8,16,8,768]{3,2,1,0:T(8,128)(2,1)}), bf16[8,16,8,768]{3,2,1,0:T(8,128)(2,1)}, u32[]{:S(2)}, u32[]{:S(2)}) async-start(bf16[8,16,8,768]{3,2,1,0:T(8,128)(2,1)} %param.24), calls=%async_computation.5 | async-start | bytes 3145728 | tf_op jit(solution)/shard_map/all_to_all | solution.py:637
  115.9 34.2 %copy-start.69 = (bf16[768]{0:T(1024)(128)(2,1)S(1)}, bf16[768]{0:T(1024)(128)(2,1)}, u32[]{:S(2)}) copy-start(bf16[768]{0:T(1024)(128)(2,1)} %param.30) | copy-start | bytes 4612
  115.9 34.8 %copy-start.70 = (bf16[768]{0:T(1024)(128)(2,1)S(1)}, bf16[768]{0:T(1024)(128)(2,1)}, u32[]{:S(2)}) copy-start(bf16[768]{0:T(1024)(128)(2,1)} %param.31) | copy-start | bytes 4612
  115.9 40.5 %copy-start.63 = (bf16[3072]{0:T(1024)(128)(2,1)S(1)}, bf16[3072]{0:T(1024)(128)(2,1)}, u32[]{:S(2)}) copy-start(bf16[3072]{0:T(1024)(128)(2,1)} %param.35) | copy-start | bytes 18436
  144.7 53.0 %all-to-all-start.3 = ((bf16[8,16,8,768]{3,2,1,0:T(8,128)(2,1)}), bf16[8,16,8,768]{3,2,1,0:T(8,128)(2,1)}, u32[]{:S(2)}, u32[]{:S(2)}) async-start(bf16[8,16,8,768]{3,2,1,0:T(8,128)(2,1)} %bitcast.127), calls=%async_computation.3 | async-start | bytes 3145728 | tf_op jit(solution)/shard_map/all_to_all | solution.py:637
  149.0 364.6 %reduce-scatter.14.cloned.1.call-start = ((), (), s32[]{:S(2)}) async-start(), calls=%async_computation.16 | async-start | bytes 10948608 | tf_op jit(solution)/shard_map/reduce_scatter | solution.py:673
  169.4 16.4 %copy-start.37 = (pred[32,32]{1,0:T(8,128)(4,1)}, pred[32,32]{1,0:T(8,128)(4,1)S(1)}, u32[]{:S(2)}) copy-start(pred[32,32]{1,0:T(8,128)(4,1)S(1)} %copy.121) | copy-start | bytes 3076
  170.2 15.6 %copy-start.39 = (pred[32,32]{1,0:T(8,128)(4,1)}, pred[32,32]{1,0:T(8,128)(4,1)S(1)}, u32[]{:S(2)}) copy-start(pred[32,32]{1,0:T(8,128)(4,1)S(1)} %copy.126) | copy-start | bytes 3076
  170.9 14.9 %copy-start.41 = (pred[32,32]{1,0:T(8,128)(4,1)}, pred[32,32]{1,0:T(8,128)(4,1)S(1)}, u32[]{:S(2)}) copy-start(pred[32,32]{1,0:T(8,128)(4,1)S(1)} %copy.127) | copy-start | bytes 3076
  171.7 14.1 %copy-start.43 = (pred[32,32]{1,0:T(8,128)(4,1)}, pred[32,32]{1,0:T(8,128)(4,1)S(1)}, u32[]{:S(2)}) copy-start(pred[32,32]{1,0:T(8,128)(4,1)S(1)} %copy.128) | copy-start | bytes 3076
  207.6 32.9 %copy-start.13 = (f32[2,16,4,8,768]{4,3,2,1,0:T(8,128)}, f32[2,16,4,8,768]{4,3,2,1,0:T(8,128)S(1)}, u32[]{:S(2)}) copy-start(f32[2,16,4,8,768]{4,3,2,1,0:T(8,128)S(1)} %copy.123) | copy-start | bytes 9437188
  215.1 25.3 %copy-start.1 = (bf16[1024,768]{1,0:T(8,128)(2,1)}, bf16[1024,768]{1,0:T(8,128)(2,1)S(1)}, u32[]{:S(2)}) copy-start(bf16[1024,768]{1,0:T(8,128)(2,1)S(1)} %get-tuple-element.141.q_ref) | copy-start | bytes 4718596
  216.5 23.9 %copy-start.67 = (f32[768]{0:T(1024)S(1)}, f32[768]{0:T(1024)}, u32[]{:S(2)}) copy-start(f32[768]{0:T(1024)} %convert_element_type.208) | copy-start | bytes 9220
  244.4 12.8 %slice-start = ((s8[4718592]{0:T(1024)(128)(4,1)}), s8[4194304]{0:T(1024)(128)(4,1)S(1)}, s32[]{:S(2)}) async-start(s8[4718592]{0:T(1024)(128)(4,1)} %bitcast.137), calls=%async_computation.18 | async-start | bytes 8388608
  282.0 299.7 %reduce-scatter.8.cloned.1.call-start = ((), (), s32[]{:S(2)}) async-start(), calls=%async_computation.13 | async-start | bytes 1216512 | tf_op jit(solution)/shard_map/reduce_scatter | solution.py:673
  297.8 15.6 %copy-start.60 = (f32[3072]{0:T(1024)S(1)}, f32[3072]{0:T(1024)}, u32[]{:S(2)}) copy-start(f32[3072]{0:T(1024)} %convert_element_type.212) | copy-start | bytes 36868
  313.4 26.8 %copy-start.19 = (f32[1024,768]{1,0:T(8,128)}, f32[1024,768]{1,0:T(8,128)S(1)}, u32[]{:S(2)}) copy-start(f32[1024,768]{1,0:T(8,128)S(1)} %fusion.62) | copy-start | bytes 9437188
  313.4 14.0 %copy-start.18 = (f32[1024,768]{1,0:T(8,128)S(1)}, f32[1024,768]{1,0:T(8,128)}, u32[]{:S(2)}) copy-start(f32[1024,768]{1,0:T(8,128)} %copy-done.17) | copy-start | bytes 9437188
  389.0 269.8 %reduce-scatter.6.cloned.1.call-start = ((), (), s32[]{:S(2)}) async-start(), calls=%async_computation.12 | async-start | bytes 3649536 | tf_op jit(solution)/shard_map/reduce_scatter | solution.py:673
  400.2 369.8 %reduce-scatter.10.cloned.1.call-start = ((), (), s32[]{:S(2)}) async-start(), calls=%async_computation.14 | async-start | bytes 4866048 | tf_op jit(solution)/shard_map/reduce_scatter | solution.py:673
  411.4 471.0 %reduce-scatter.12.cloned.1.call-start = ((), (), s32[]{:S(2)}) async-start(), calls=%async_computation.15 | async-start | bytes 4866048 | tf_op jit(solution)/shard_map/reduce_scatter | solution.py:673
  412.9 19.4 %slice-start.4 = ((s8[6291456]{0:T(1024)(128)(4,1)}), s8[4194304]{0:T(1024)(128)(4,1)S(1)}, s32[]{:S(2)}) async-start(s8[6291456]{0:T(1024)(128)(4,1)} %bitcast.141), calls=%async_computation.22 | async-start | bytes 8388608
  464.8 44.5 %all-to-all-start.4 = ((bf16[8,16,8,768]{3,2,1,0:T(8,128)(2,1)}), bf16[8,16,8,768]{3,2,1,0:T(8,128)(2,1)}, u32[]{:S(2)}, u32[]{:S(2)}) async-start(bf16[8,16,8,768]{3,2,1,0:T(8,128)(2,1)} %bitcast.114), calls=%async_computation.4 | async-start | bytes 3145728 | tf_op jit(solution)/shard_map/all_to_all | solution.py:648
  483.8 32.3 %copy-start.72 = (u32[32]{0:T(128)S(1)}, u32[32]{0:T(128)}, u32[]{:S(2)}) copy-start(u32[32]{0:T(128)} %constant.83) | copy-start | bytes 388
  485.0 38.2 %copy-start.62 = (bf16[768]{0:T(1024)(128)(2,1)S(1)}, bf16[768]{0:T(1024)(128)(2,1)}, u32[]{:S(2)}) copy-start(bf16[768]{0:T(1024)(128)(2,1)} %get-tuple-element.136) | copy-start | bytes 4612
  485.0 38.8 %copy-start.61 = (bf16[768]{0:T(1024)(128)(2,1)S(1)}, bf16[768]{0:T(1024)(128)(2,1)}, u32[]{:S(2)}) copy-start(bf16[768]{0:T(1024)(128)(2,1)} %get-tuple-element.142) | copy-start | bytes 4612
  509.2 79.3 %all-to-all-start.6 = ((bf16[8,16,8,768]{3,2,1,0:T(8,128)(2,1)}), bf16[8,16,8,768]{3,2,1,0:T(8,128)(2,1)}, u32[]{:S(2)}, u32[]{:S(2)}) async-start(bf16[8,16,8,768]{3,2,1,0:T(8,128)(2,1)} %bitcast.109), calls=%async_computation.6 | async-start | bytes 3145728 | tf_op jit(solution)/shard_map/all_to_all | solution.py:648
  513.6 387.6 %all-gather.2.cloned.1.call-start = ((), (), s32[]{:S(2)}) async-start(), calls=%async_computation.17 | async-start | bytes 1658880 | tf_op jit(solution)/shard_map/all_gather | solution.py:676
  (61 other events, 212.8 us)
Sparse Core Ops, SparseCore 0:
  282.2 143.1 reduce-scatter.13
  431.1 120.3 reduce-scatter.7
  556.9 101.8 reduce-scatter.5
  664.1 105.8 reduce-scatter.9
  776.2 106.0 reduce-scatter.11
  883.8 17.3 all-gather.1

commit v2 on v1

--- a/solution.py
+++ b/solution.py
@@ -605,7 +605,7 @@
     )(queries, key_rows, values, columns, key_marks, out, grad)
 
 
-def fetch_codes(code_ids, embed_table):
+def fetch_codes(code_ids, embed_table, first):
     features = embed_table.shape[1]
     holder_count = lax.axis_size(("ty", "tx"))
     share_rows = embed_table.shape[0]
@@ -626,6 +626,7 @@
     requests = requests.reshape(holder_count, slot_count)
     asked = lax.all_to_all(requests, ("ty", "tx"), split_axis=0, concat_axis=0, tiled=True)
     fetched = embed_table.at[asked.reshape(-1)].get(mode="promise_in_bounds")
+    fetched, _ = lax.optimization_barrier((fetched, first))
     fetched = fetched.reshape(holder_count, slot_count, features)
     returned = lax.all_to_all(fetched, ("ty", "tx"), split_axis=0, concat_axis=0, tiled=True)
     returned = returned.reshape(holder_count * slot_count, features)
@@ -648,19 +649,99 @@
     return lax.all_to_all(parts, ("ty", "tx"), split_axis=0, concat_axis=0, tiled=True)
 
 
-def neighbours(rows_grid, marks_grid, direction):
+def conv_kernel(rows_ref, mask_ref, weight_ref, bias_ref, *refs, width, sign):
+    if sign > 0:
+        out_ref, shifted, total = refs
+    else:
+        out_ref, low_ref, taps_ref, shifted, total = refs
+    tap = pl.program_id(0)
+    tokens, features = rows_ref.shape
+
+    @pl.when(tap == 0)
+    def _():
+        total[...] = jnp.zeros_like(total)
+        rows = rows_ref[...]
+        for j in range(3):
+            moved = rows
+            if j != 1:
+                moved = pltpu.roll(rows.astype(jnp.float32), (1 - j) % tokens, 0)
+            shifted[j, 0:width, :] = jnp.zeros((width, features), jnp.bfloat16)
+            shifted[j, width + tokens :, :] = jnp.zeros((width, features), jnp.bfloat16)
+            shifted[j, width : width + tokens, :] = moved.astype(jnp.bfloat16)
+
+    down, right = tap // 3, tap % 3
+    if sign < 0:
+        down, right = 2 - down, 2 - right
+    step = tokens // 4
+    for i in range(4):
+        rows = slice(i * step, (i + 1) * step)
+        first = pl.multiple_of(down * width + i * step, width)
+        mask = jnp.concatenate([mask_ref[0, rows, :]] * (features // 128), axis=1)
+        taken = shifted[right, pl.ds(first, step), :] * mask
+        if sign < 0:
+            taps_ref[rows, :] = taken
+            total[rows, :] += nt(taken, weight_ref[0])
+        else:
+            total[rows, :] += nn(taken, weight_ref[0])
+
+    @pl.when(tap == 8)
+    def _():
+        if sign > 0:
+            out_ref[...] = (total[...] + bias_ref[...].astype(jnp.float32)).astype(jnp.bfloat16)
+        else:
+            out_ref[...] = total[...]
+            low_ref[...] = total[...].astype(jnp.bfloat16)
+
+
+def conv(rows, masks, weight, bias, width, sign):
+    tokens, features = rows.shape
+
+    def whole(shape):
+        return pl.BlockSpec(shape, lambda k: (0, 0))
+
+    low = jax.ShapeDtypeStruct((tokens, features), jnp.bfloat16)
+    out_shape, out_specs = low, whole((tokens, features))
+    if sign < 0:
+        taps = jax.ShapeDtypeStruct((tokens, 9 * features), jnp.bfloat16)
+        out_shape = [jax.ShapeDtypeStruct((tokens, features), jnp.float32), low, taps]
+        out_specs = [out_specs, out_specs, pl.BlockSpec((tokens, features), lambda k: (0, k))]
+    tap_of = (lambda k: (k, 0, 0)) if sign > 0 else (lambda k: (8 - k, 0, 0))
+    return pl.pallas_call(
+        partial(conv_kernel, width=width, sign=sign),
+        grid=(9,),
+        in_specs=[
+            whole((tokens, features)),
+            pl.BlockSpec((1, tokens, 128), tap_of),
+            pl.BlockSpec((1, features, features), lambda k: (k, 0, 0)),
+            whole((1, features)),
+        ],
+        out_specs=out_specs,
+        out_shape=out_shape,
+        scratch_shapes=[
+            pltpu.VMEM((3, tokens + 2 * width, features), jnp.bfloat16),
+            pltpu.VMEM((tokens, features), jnp.float32),
+        ],
+        compiler_params=pltpu.CompilerParams(vmem_limit_bytes=48 * 2**20),
+        cost_estimate=pl.CostEstimate(
+            flops=18 * tokens * features * features,
+            bytes_accessed=18 * features * features + 4 * tokens * features,
+            transcendentals=0,
+        ),
+        name="conv",
+    )(rows, masks, weight, bias)
+
+
+def tap_masks(marks_grid):
     height, width = marks_grid.shape
-    padded = jnp.pad(rows_grid, ((1, 1), (1, 1), (0, 0)))
-    marks_pad = jnp.pad(marks_grid, ((1, 1), (1, 1)), constant_values=-1)
-    taps = []
-    for vertical in range(3):
-        for lateral in range(3):
-            down = vertical if direction > 0 else 2 - vertical
-            right = lateral if direction > 0 else 2 - lateral
-            inside = marks_pad[down : down + height, right : right + width] == marks_grid
-            rows = padded[down : down + height, right : right + width]
-            taps.append(jnp.where(inside[..., None], rows, 0).reshape(height * width, -1))
-    return jnp.concatenate(taps, axis=1)
+    padded = jnp.pad(marks_grid, ((1, 1), (1, 1)), constant_values=-1)
+    masks = jnp.stack(
+        [
+            (padded[a : a + height, b : b + width] == marks_grid).reshape(height * width)
+            for a in range(3)
+            for b in range(3)
+        ]
+    ).astype(jnp.bfloat16)
+    return jnp.broadcast_to(masks[:, :, None], (9, height * width, 128))
 
 
 def gelu_parts(values):
@@ -669,11 +750,171 @@
     return values * upto, upto + values * spread * 0.3989422804014327
 
 
-def sum_shares(grad):
-    shares = lax.psum_scatter(
-        grad.astype(jnp.bfloat16), ("ty", "tx", "gr"), scatter_dimension=0, tiled=True
-    )
-    return lax.all_gather(shares, "gr", axis=0, tiled=True).astype(jnp.float32)
+def sum_kernel(*refs, layout, count, lead):
+    ins = refs[: max(item[0] for item in layout) + 1]
+    out = refs[len(ins)]
+    (own, got0, got1, got2, got3, got4, whole) = refs[len(ins) + 1 : len(ins) + 8]
+    (own_sem, s0, r0, s1, r1, s2, r2, s3, r3, s4, r4, s5, r5, s6, r6, out_sem) = refs[len(ins) + 8 :]
+    gr, ty, tx = lax.axis_index("gr"), lax.axis_index("ty"), lax.axis_index("tx")
+    x, core, half, par = gr // 2, gr % 2, tx // 2, tx % 2
+    mate = (2 * x + 1 - core, ty, tx)
+    over_x = (2 * (1 - x) + core, ty, tx)
+    over_y = (gr, 1 - ty, tx)
+    near = (gr, ty, half * 2 + (1 - par))
+    away = (gr, ty, (1 - half) * 2 + par)
+    barrier = pltpu.get_barrier_semaphore()
+    for device in (mate, over_x, over_y, near, away):
+        pl.semaphore_signal(barrier, inc=1, device_id=device, device_id_type=pl.DeviceIdType.MESH)
+    pl.semaphore_wait(barrier, 5)
+    width = own.shape[-1]
+    own_columns = pl.ds(pl.multiple_of(core * width, 128), width)
+
+    def part(block, which):
+        source, prefix, column = layout[block]
+        columns = pl.ds(pl.multiple_of(column + which * width, 128), width)
+        if prefix is None:
+            return ins[source].at[:, :, :, :, :, columns]
+        return ins[source].at[:, :, :, prefix, :, :, columns]
+
+    def put(source, target, sent, received, device):
+        return pltpu.make_async_remote_copy(
+            src_ref=source,
+            dst_ref=target,
+            send_sem=sent,
+            recv_sem=received,
+            device_id=device,
+            device_id_type=pl.DeviceIdType.MESH,
+        )
+
+    for block in range(2 * count):
+        put(part(block, 1 - core), got0.at[block], s0.at[block], r0.at[block], mate).start()
+        pltpu.make_async_copy(part(block, core), own.at[block], own_sem.at[block]).start()
+
+    def level0(b):
+        return put(got0.at[b], got0.at[b], s0.at[b], r0.at[b], mate)
+
+    def level1x(c):
+        return put(own.at[2 * c, :, :, :, 1 - x], got1.at[c, 0], s1.at[c, 0], r1.at[c, 0], over_x)
+
+    def level1y(c):
+        return put(own.at[2 * c + 1, 1 - ty], got1.at[c, 1], s1.at[c, 1], r1.at[c, 1], over_y)
+
+    def level2y(c):
+        return put(got1.at[c, 0, 1 - ty], got2.at[c, 0], s2.at[c, 0], r2.at[c, 0], over_y)
+
+    def level2x(c):
+        return put(got1.at[c, 1, :, :, 1 - x], got2.at[c, 1], s2.at[c, 1], r2.at[c, 1], over_x)
+
+    def level3(c):
+        return put(got2.at[c, :, :, 1 - par], got3.at[c], s3.at[c], r3.at[c], near)
+
+    def level4(c):
+        return put(got3.at[c, :, 1 - half], got4.at[c], s4.at[c], r4.at[c], away)
+
+    def level5(c):
+        place = whole.at[pl.ds(2 * c, 2), x, :, own_columns]
+        return put(place, place, s5.at[c], r5.at[c], over_x)
+
+    def level6(c):
+        place = whole.at[pl.ds(2 * c, 2), :, :, own_columns]
+        return put(place, place, s6.at[c], r6.at[c], mate)
+
+    def stage1(c):
+        for b in (2 * c, 2 * c + 1):
+            level0(b).wait_recv()
+            pltpu.make_async_copy(own.at[b], own.at[b], own_sem.at[b]).wait()
+
+            def add(i, _):
+                y, h, p = i // 4, (i // 2) % 2, i % 2
+                own[b, y, h, p] = own[b, y, h, p] + got0[b, y, h, p]
+                return 0
+
+            lax.fori_loop(0, 8, add, 0)
+        level1x(c).start()
+        level1y(c).start()
+
+    def stage2(c):
+        level1x(c).wait_recv()
+        got1[c, 0] = got1[c, 0] + own[2 * c, :, :, :, x]
+        level2y(c).start()
+        level1y(c).wait_recv()
+        got1[c, 1] = got1[c, 1] + own[2 * c + 1, ty]
+        level2x(c).start()
+
+    def stage3(c):
+        level2y(c).wait_recv()
+        level2x(c).wait_recv()
+        got2[c, 0] = got2[c, 0] + got1[c, 0, ty]
+        got2[c, 1] = got2[c, 1] + got1[c, 1, :, :, x]
+        level3(c).start()
+
+    def stage4(c):
+        level3(c).wait_recv()
+        got3[c] = got3[c] + got2[c, :, :, par]
+        level4(c).start()
+
+    def stage5(c):
+        level4(c).wait_recv()
+        whole[pl.ds(2 * c, 2), x, :, own_columns] = got4[c] + got3[c, :, half]
+        level5(c).start()
+
+    def stage6(c):
+        level5(c).wait_recv()
+        level6(c).start()
+
+    stages = (stage1, stage2, stage3, stage4, stage5, stage6)
+
+    def turn(t, _):
+        for stage, behind in zip(stages, lead):
+            c = t - behind
+            pl.when((c >= 0) & (c < count))(partial(stage, c))
+        return 0
+
+    lax.fori_loop(0, count + lead[-1], turn, 0)
+
+    def finish(c, _):
+        level6(c).wait_recv()
+        level0(2 * c).wait_send()
+        level0(2 * c + 1).wait_send()
+        for level in (level1x, level1y, level2x, level2y, level3, level4, level5, level6):
+            level(c).wait_send()
+        return 0
+
+    lax.fori_loop(0, count, finish, 0)
+    done = pltpu.make_async_copy(whole, out, out_sem)
+    done.start()
+    done.wait()
+
+
+def sum_blocks(ins, layout, collective_id):
+    blocks = len(layout)
+    count = blocks // 2
+    rows, width = ins[0].shape[-2], 384
+    dma = pltpu.SemaphoreType.DMA
+    half_block = pltpu.VMEM((blocks, 2, 2, 2, 2, rows, width), jnp.bfloat16)
+    return pl.pallas_call(
+        partial(sum_kernel, layout=layout, count=count, lead=(0, 2, 4, 6, 8, 10)),
+        in_specs=[pl.BlockSpec(memory_space=pl.ANY)] * len(ins),
+        out_specs=pl.BlockSpec(memory_space=pl.ANY),
+        out_shape=jax.ShapeDtypeStruct((blocks, 2, rows, 2 * width), jnp.bfloat16),
+        scratch_shapes=[
+            half_block,
+            half_block,
+            pltpu.VMEM((count, 2, 2, 2, 2, rows, width), jnp.bfloat16),
+            pltpu.VMEM((count, 2, 2, 2, rows, width), jnp.bfloat16),
+            pltpu.VMEM((count, 2, 2, rows, width), jnp.bfloat16),
+            pltpu.VMEM((count, 2, rows, width), jnp.bfloat16),
+            pltpu.VMEM((blocks, 2, rows, 2 * width), jnp.bfloat16),
+        ]
+        + [dma((blocks,))] * 3
+        + [dma((count, 2))] * 4
+        + [dma((count,))] * 8
+        + [dma],
+        compiler_params=pltpu.CompilerParams(
+            collective_id=collective_id, has_side_effects=True, vmem_limit_bytes=56 * 2**20
+        ),
+        name="sum_blocks",
+    )(*ins)
 
 
 def on_device_grids(
@@ -704,15 +945,16 @@
     cotangent_grid = to_grid(recon_grad)
     height, width = marks_grid.shape
     tokens = height * width
-    codes_tile = fetch_codes(code_ids, embed_table).reshape(encoder_out.shape)
+    codes_tile = fetch_codes(code_ids, embed_table, cotangent_grid).reshape(encoder_out.shape)
     start_rows = to_grid(codes_tile).reshape(tokens, features).astype(wide)
     query_marks, key_marks = mark_columns(marks_grid.reshape(tokens))
 
+    masks = tap_masks(marks_grid)
     cotangent = cotangent_grid.reshape(tokens, features)
-    behind = neighbours(cotangent_grid, marks_grid, -1)
-    pixel_flat = pixel_weight.reshape(features, 9 * features)
-    final_grad = right_product(behind, pixel_flat)
-    lower_grad = final_grad.astype(jnp.bfloat16)
+    pixel_taps = jnp.swapaxes(pixel_weight, 0, 1)
+    final_grad, lower_grad, behind = conv(
+        cotangent, masks, pixel_taps, pixel_bias.reshape(1, features), width, -1
+    )
     pixel_bias_grad = jnp.sum(cotangent.astype(wide), axis=0)
     down_bias_grad = jnp.sum(lower_grad.astype(wide), axis=0)
     hidden_grad = right_product(lower_grad, down_weight)
@@ -740,15 +982,13 @@
     output_rows = middle + (matmul(hidden_low, down_weight) + down_bias.astype(wide))
     features_low = output_rows.astype(jnp.bfloat16)
 
+    recon_rows = conv(features_low, masks, pixel_taps, pixel_bias.reshape(1, features), width, 1)
+    recon_tiles = to_tiles(recon_rows.reshape(height, width, features))
+
     pixel_weight_grad = left_product(features_low, behind)
     down_weight_grad = left_product(hidden_low, lower_grad)
     up_weight_grad = left_product(normed_two_low, pre_grad)
     up_bias_grad = jnp.sum(pre_grad.astype(wide), axis=0)
-
-    ahead = neighbours(features_low.reshape(height, width, features), marks_grid, 1)
-    pixel_rows = jnp.swapaxes(pixel_weight, 0, 1).reshape(9 * features, features)
-    recon_grid = (matmul(ahead, pixel_rows) + pixel_bias.astype(wide)).astype(jnp.bfloat16)
-    recon_tiles = to_tiles(recon_grid.reshape(height, width, features))
 
     middle_part, second_gain_grad, second_shift_grad = second_pull(
         right_product(pre_grad, up_weight)
@@ -788,8 +1028,31 @@
         pixel_bias_grad,
     ]
     shards = lax.axis_size(("ty", "tx"))
-    packed = jnp.concatenate([v.reshape(shards, -1) for v in vectors], axis=1).reshape(-1)
-    packed = sum_shares(packed)
+    rows = features // shards
+    packed = jnp.concatenate([v.reshape(shards, -1) for v in vectors], axis=1)
+    packed = jnp.pad(packed, ((0, 0), (0, rows * features - packed.shape[1])))
+    spread = (2, 2, 2)
+
+    def cut(grad):
+        split = spread + ((grad.shape[0] // features,) if grad.shape[0] > features else ())
+        return grad.astype(jnp.bfloat16).reshape(split + (2, rows // 2, grad.shape[1]))
+
+    ins = [
+        cut(pixel_weight_grad),
+        cut(up_weight_grad),
+        cut(down_weight_grad),
+        cut(out_weight_grad),
+        cut(qkv_weight_grad),
+        cut(packed.reshape(features, features)),
+    ]
+    layout = [(0, None, features * k) for k in range(9)]
+    layout += [(1, None, features * k) for k in range(4)]
+    layout += [(2, k, 0) for k in range(4)]
+    layout += [(3, None, 0)]
+    layout += [(4, None, features * k) for k in range(3)]
+    layout += [(5, None, 0)]
+    summed = sum_blocks(ins, layout, 1).reshape(len(layout), rows, features).astype(wide)
+    packed = summed[21].reshape(-1)
     sums = []
     at = 0
     for vector in vectors:
@@ -801,20 +1064,20 @@
     return (
         recon_tiles,
         input_tiles,
-        sum_shares(qkv_weight_grad),
+        jnp.swapaxes(summed[18:21], 0, 1).reshape(rows, 3 * features),
         query_bias_sum,
         value_bias_sum,
-        sum_shares(out_weight_grad),
+        summed[17],
         out_bias_sum,
         first_gain_sum,
         first_shift_sum,
         second_gain_sum,
         second_shift_sum,
-        sum_shares(up_weight_grad),
+        jnp.swapaxes(summed[9:13], 0, 1).reshape(rows, 4 * features),
         up_bias_sum,
-        sum_shares(down_weight_grad),
+        summed[13:17].reshape(4 * rows, features),
         down_bias_sum,
-        sum_shares(pixel_weight_grad).reshape(-1, 9, features),
+        jnp.swapaxes(summed[0:9], 0, 1),
         pixel_bias_sum,
     )
 
@@ -863,7 +1126,7 @@
     )
     def on_device(encoder_out, *rest):
         members = mesh.shape["ty"] * mesh.shape["tx"]
-        whole_grids = encoder_out.shape[0] == members
+        whole_grids = encoder_out.shape[0] == members and tuple(mesh.devices.shape) == (4, 2, 4)
         body = on_device_grids if whole_grids else on_device_bands
         return body(encoder_out, *rest)
 

time: 925 us -> 633 us (0.68)
  waiting for transfers between devices: 342 us -> 39.5 us
  Pallas kernels: 61 us -> 237 us
  blocking collectives: 136 us -> 59.1 us
  matrix products: 135 us -> 102 us
  local copies, waits for them, and re-layouts: 133 us -> 107 us
  between operations: 16.7 us -> 1.89 us
  other arithmetic: 62.4 us -> 48.1 us
    reduce_scatter x5 -> x0, waiting for transfers between devices: 274 us -> none  [sum_shares(): lax.psum_scatter(grad.astype(jnp.bfloat16), ('ty', 'tx', 'gr'), scatter_d...]
    pallas_call x0 -> x3, Pallas kernels: none -> 175 us  [the longest x1 139 us: sum_blocks(): pl.pallas_call(partial(sum_kernel, layout=layout, count=count, lead=(0, 2...]
    unnamed x190 -> x105, local copies, waits for them, and re-layouts: 67 us -> 15.1 us
    unnamed x2 -> x0, blocking collectives: 48.7 us -> none
    all_gather x4 -> x0, blocking collectives: 28.1 us -> none  [sum_shares(): return lax.all_gather(shares, 'gr', axis=0, tiled=True).astype(jnp.float32)]
    dot_general x5 -> x4, matrix products: 51.2 us -> 31.5 us  [right_product(): lax.dot_general(left_side, right_side, (((1,), (1,)), ((), ())), preferre...]
    all_to_all x2, waiting for transfers between devices: 24.2 us -> 5.59 us  [to_tiles(): lax.all_to_all(parts, ('ty', 'tx'), split_axis=0, concat_axis=0, tiled=True)]
    select_n x2 -> x0, other arithmetic: 17.8 us -> none  [neighbours(): jnp.where(inside[..., None], rows, 0).reshape(height * width, -1)]
  transfers between devices with their start and end apart: 12 -> 6, of which waited for: 7 -> 3; matrix products, arithmetic and copies ran while one was open for 26% -> 23% of each run, Pallas kernels for 4% -> 25%
where the time goes in v2:
time: 633 us; the launch traced here: 625 us
  Pallas kernels  237 us (37%)
  local copies, waits for them, and re-layouts  107 us (17%)
  matrix products  102 us (16%)
  blocking collectives  59.1 us (9%)
  other arithmetic  48.1 us (8%)
  waiting for transfers between devices  39.5 us (6%)
  starting transfers between devices  30.9 us (5%)
    pallas_call x1, Pallas kernels, sum_blocks(): pl.pallas_call(partial(sum_kernel, layout=layout, count=count, lead=(0, 2...  139 us
    all_to_all x1, blocking collectives, fetch_codes(): lax.all_to_all(fetched, ('ty', 'tx'), split_axis=0, concat_axis=0, tiled=...  59.1 us
    dot_general x5, matrix products, left_product(): lax.dot_general(left_side, right_side, (((0,), (0,)), ((), ())), preferre...  48.3 us
    pallas_call x1, Pallas kernels, attend_back_grid(): pl.pallas_call(partial(attend_back_kernel, step=min(512, tokens)), grid=(...  37.2 us
    pallas_call x2, Pallas kernels, conv(): pl.pallas_call(partial(conv_kernel, width=width, sign=sign), grid=(9,), i...  36 us
    dot_general x4, matrix products, right_product(): lax.dot_general(left_side, right_side, (((1,), (1,)), ((), ())), preferre...  31.5 us
    all_to_all x3, waiting for transfers between devices, to_grid(): lax.all_to_all(tiles, ('ty', 'tx'), split_axis=0, concat_axis=0, tiled=True)  28.8 us
    pallas_call x1, Pallas kernels, attend(): pl.pallas_call(attend_kernel, grid=(features // 128,), in_specs=[pair, pa...  24.6 us
  transfers between devices with their start and end apart: 6, of which 3 were waited for; matrix products, arithmetic and copies ran while one was open for 23% of the time, Pallas kernels for 25%

profile of v2, /device:TPU:0, one launch (start us, length us, event | category | flops | bytes accessed | tf_op | source)
XLA Modules:
  0.0 625.2 jit_solution(11721545993880712538)
XLA Ops:
  3.8 4.3 scatter_custom_fusion
  8.8 7.3 %all-to-all-start = ((s32[8,1,192]{2,1,0:T(1,128)}), s32[8,1,192]{2,1,0:T(1,128)S(1)}, u32[]{:S(2)}, u32[]{:S(2)}) async-start(s32[8,1,192]{2,1,0:T(1,128)} %all_to_all.24), calls=%async_computation | async-start | bytes 16384 | tf_op jit(solution)/shard_map/all_to_all | solution.py:627
  17.6 5.1 all-to-all-done
  22.7 3.9 all-to-all-start.3
  26.7 11.7 %gather_fusion = bf16[1536,768]{1,0:T(8,128)(2,1)} fusion(bf16[6284,768]{1,0:T(8,128)(2,1)} %param.23, s32[2048]{0:T(1024)S(1)} %pad_clamp_fusion), kind=kCustom, calls=%fused_computation | custom fusion | bytes 4724736 | tf_op jit(solution)/shard_map/gather | solution.py:628
  38.4 59.1 %all_to_all.39 = bf16[8,192,768]{2,1,0:T(8,128)(2,1)} all-to-all(bf16[8,192,768]{2,1,0:T(8,128)(2,1)} %bitcast.108), channel_id=1, replica_groups=mesh['gr'=4,'ty'=2,'tx'=4] {'ty','tx'}, dimensions={0} | all-to-all | bytes 4718592 | tf_op jit(solution)/shard_map/all_to_all | solution.py:631
  97.6 4.3 all-to-all-start.5
  101.9 7.5 %gather_fusion.1 = bf16[1024,768]{1,0:T(8,128)(2,1)} fusion(bf16[1536,768]{1,0:T(8,128)(2,1)} %bitcast.106, s32[1024]{0:T(1024)S(1)} %broadcast_clamp_fusion), kind=kCustom, calls=%fused_computation.1 | custom fusion | bytes 3149824 | tf_op jit(solution)/shard_map/gather | solution.py:633
  109.4 28.8 %all-to-all-done.5 = bf16[8,16,8,768]{3,2,1,0:T(8,128)(2,1)} async-done(((bf16[8,16,8,768]{3,2,1,0:T(8,128)(2,1)}), bf16[8,16,8,768]{3,2,1,0:T(8,128)(2,1)}, u32[]{:S(2)}, u32[]{:S(2)}) %all-to-all-start.5) | async-done | bytes 1572896 | tf_op jit(solution)/shard_map/all_to_all | solution.py:638
  138.2 4.5 all-to-all-start.2
  192.6 20.3 %conv.3 = (f32[1024,768]{1,0:T(8,128)}, bf16[1024,768]{1,0:T(8,128)(2,1)S(1)}, bf16[1024,6912]{1,0:T(8,128)(2,1)}) custom-call(bf16[1024,768]{1,0:T(8,128)(2,1)S(1)} %bitcast.104, bf16[9,1024,128]{2,1,0:T(8,128)(2,1)S(1)} %broadcast_in_dim.30.mask_ref, bf16[9,768,768]{2,1,0:T(8,128)(2,1)} %bitcast.134, bf16[1,768]{1,0:T(2,128)(2,1)S(1)} %reshape.409.bias_ref), custom_call_target="tpu_custom_call" | custom-call | flops 10871635968 | bytes 13762560 | tf_op jit(solution)/shard_map/conv/pallas_call | solution.py:709
  229.1 3.8 fusion.45
  236.0 24.6 %attend.1 = (bf16[1024,768]{1,0:T(8,128)(2,1)S(1)}, bf16[1024,768]{1,0:T(8,128)(2,1)S(1)}) custom-call(bf16[1024,768]{1,0:T(8,128)(2,1)S(1)} %get-tuple-element.45.q_ref, bf16[1024,768]{1,0:T(8,128)(2,1)} %get-tuple-element.44.k_ref, bf16[1024,768]{1,0:T(8,128)(2,1)} %fusion.7.v_ref, bf16[1024,128]{1,0:T(8,128)(2,1)S(1)} %copy-done.8, ...), custom_call_target="tpu_custom_call" | custom-call | flops 12884901888 | bytes 7864320 | tf_op jit(solution)/shard_map/attend/pallas_call | solution.py:519
  265.2 11.8 %multiply_convert_fusion = (bf16[1024,3072]{1,0:T(8,128)(2,1)}, f32[1024,3072]{1,0:T(8,128)}) fusion(f32[3072]{0:T(1024)S(1)} %copy-done.32, bf16[768,3072]{1,0:T(8,128)(2,1)S(1)} %bitcast.137, f32[1024,768]{1,0:T(8,128)S(1)} %get-tuple-element.76, f32[768]{0:T(1024)S(1)} %copy-done.36, f32[768]{0:T(1024)S(1)} %copy-done.27, f32[1024]{0:T(1024)S(1)} %fusion.31, ...), kind=kOutput, calls=%fused_computation.10 | convolution fusion | flops 4854644736 | bytes 26765312 | tf_op jit(solution)/shard_map/dot_general | solution.py:42
  277.0 14.2 %fusion.44 = (bf16[3072]{0:T(1024)(128)(2,1)}, bf16[1024,3072]{1,0:T(8,128)(2,1)}) fusion(f32[1024,3072]{1,0:T(8,128)} %get-tuple-element.78, f32[3072]{0:T(1024)S(1)} %copy-done.32, bf16[1024,768]{1,0:T(8,128)(2,1)S(1)} %copy-done.5, bf16[3072,768]{1,0:T(8,128)(2,1)} %param.36), kind=kOutput, calls=%fused_computation.110 | convolution fusion | flops 4869583872 | bytes 25184256 | tf_op jit(solution)/shard_map/dot_general | solution.py:52
  291.2 8.4 %multiply_reduce_fusion = (bf16[768]{0:T(1024)(128)(2,1)}, f32[1024]{0:T(1024)S(1)}, bf16[768]{0:T(1024)(128)(2,1)}, f32[1024,768]{1,0:T(8,128)S(1)}) fusion(f32[1024,768]{1,0:T(8,128)S(1)} %get-tuple-element.76, f32[1024]{0:T(1024)S(1)} %fusion.31, f32[1024]{0:T(1024)S(1)} %broadcast_multiply_fusion.1, f32[768]{0:T(1024)S(1)} %copy-done.27, ...), kind=kOutput, calls=%fused_computation.31 | convolution fusion | flops 4838126592 | bytes 17319936 | tf_op jit(solution)/shard_map/dot_general | solution.py:52
  299.6 10.1 %convolution_convert_fusion.2 = bf16[768,3072]{1,0:T(8,128)(2,1)} fusion(bf16[1024,3072]{1,0:T(8,128)(2,1)} %get-tuple-element.82, f32[1024,768]{1,0:T(8,128)S(1)} %get-tuple-element.76, f32[768]{0:T(1024)S(1)} %copy-done.36, f32[768]{0:T(1024)S(1)} %copy-done.27, f32[1024]{0:T(1024)S(1)} %fusion.31, f32[1024]{0:T(1024)S(1)} %broadcast_multiply_fusion.1), kind=kOutput, calls=%fused_computation.14 | convolution fusion | flops 4838129664 | bytes 14170112 | tf_op jit(solution)/shard_map/dot_general | solution.py:46
  316.2 37.2 %attend_back.1 = (bf16[1024,768]{1,0:T(8,128)(2,1)S(1)}, bf16[1024,768]{1,0:T(8,128)(2,1)S(1)}, bf16[1024,768]{1,0:T(8,128)(2,1)S(1)}) custom-call(bf16[1024,768]{1,0:T(8,128)(2,1)} %copy-done.3, bf16[1024,768]{1,0:T(8,128)(2,1)} %get-tuple-element.44.k_ref, bf16[1024,768]{1,0:T(8,128)(2,1)} %fusion.7.v_ref, bf16[1024,768]{1,0:T(8,128)(2,1)} %copy-done.12, ...), custom_call_target="tpu_custom_call" | custom-call | flops 19327352832 | bytes 14155776 | tf_op jit(solution)/shard_map/attend_back/pallas_call | solution.py:591
  355.5 5.6 convolution_convert_fusion.3
  361.2 6.2 fusion.33
  367.5 5.1 add_convert_fusion.1.rows_ref
  372.6 15.6 %conv.2 = bf16[1024,768]{1,0:T(8,128)(2,1)S(1)} custom-call(bf16[1024,768]{1,0:T(8,128)(2,1)S(1)} %add_convert_fusion.1.rows_ref, bf16[9,1024,128]{2,1,0:T(8,128)(2,1)S(1)} %copy-done.2, bf16[9,768,768]{2,1,0:T(8,128)(2,1)} %bitcast.135, bf16[1,768]{1,0:T(2,128)(2,1)S(1)} %reshape.409.bias_ref), custom_call_target="tpu_custom_call" | custom-call | flops 10871635968 | bytes 13762560 | tf_op jit(solution)/shard_map/conv/pallas_call | solution.py:709
  389.5 6.3 %all-to-all-start.4 = ((bf16[8,16,8,768]{3,2,1,0:T(8,128)(2,1)}), bf16[8,16,8,768]{3,2,1,0:T(8,128)(2,1)}, u32[]{:S(2)}, u32[]{:S(2)}) async-start(bf16[8,16,8,768]{3,2,1,0:T(8,128)(2,1)} %bitcast.110), calls=%async_computation.4 | async-start | bytes 3145728 | tf_op jit(solution)/shard_map/all_to_all | solution.py:649
  396.5 4.5 multiply_reduce_fusion.1
  401.2 3.7 fusion.10
  407.0 18.5 %convolution_convert_fusion = bf16[768,6912]{1,0:T(8,128)(2,1)} fusion(bf16[1024,768]{1,0:T(8,128)(2,1)S(1)} %copy-done.11, bf16[1024,6912]{1,0:T(8,128)(2,1)} %get-tuple-element.32), kind=kOutput, calls=%fused_computation.12 | convolution fusion | flops 10876944384 | bytes 26345472 | tf_op jit(solution)/shard_map/dot_general | solution.py:46
  425.4 5.6 all-to-all-done.4
  431.0 4.6 all-to-all-start.6
  435.6 4.3 convolution_convert_fusion.5
  453.0 9.8 %convolution_convert_fusion.1 = bf16[3072,768]{1,0:T(8,128)(2,1)} fusion(bf16[1024,3072]{1,0:T(8,128)(2,1)} %get-tuple-element.77, bf16[1024,768]{1,0:T(8,128)(2,1)S(1)} %copy-done.6), kind=kOutput, calls=%fused_computation.13 | convolution fusion | flops 4834197504 | bytes 12582912 | tf_op jit(solution)/shard_map/dot_general | solution.py:46
  462.8 138.9 %sum_blocks.1 = bf16[22,2,48,768]{3,2,1,0:T(8,128)(2,1)} custom-call(bf16[2,2,2,2,48,6912]{5,4,3,2,1,0:T(8,128)(2,1)} %bitcast.107, bf16[2,2,2,2,48,3072]{5,4,3,2,1,0:T(8,128)(2,1)} %bitcast.117, bf16[2,2,2,4,2,48,768]{6,5,4,3,2,1,0:T(8,128)(2,1)} %bitcast.118, bf16[2,2,2,2,48,768]{5,4,3,2,1,0:T(8,128)(2,1)} %bitcast.122, ...), custom_call_target="tpu_custom_call" | custom-call | tf_op jit(solution)/shard_map/sum_blocks/pallas_call | solution.py:895
  618.6 3.5 add_convert_fusion
  (216 shorter events, 124.0 us)
Async XLA Ops:
  0.7 228.4 %copy-start = (bf16[768,2304]{1,0:T(8,128)(2,1)S(1)}, bf16[768,2304]{1,0:T(8,128)(2,1)}, u32[]{:S(2)}) copy-start(bf16[768,2304]{1,0:T(8,128)(2,1)} %param.25) | copy-start | bytes 10616836
  3.8 5.0 copy-start.29
  8.8 13.8 %all-to-all-start = ((s32[8,1,192]{2,1,0:T(1,128)}), s32[8,1,192]{2,1,0:T(1,128)S(1)}, u32[]{:S(2)}, u32[]{:S(2)}) async-start(s32[8,1,192]{2,1,0:T(1,128)} %all_to_all.24), calls=%async_computation | async-start | bytes 16384 | tf_op jit(solution)/shard_map/all_to_all | solution.py:627
  22.7 15.8 %all-to-all-start.3 = ((s32[8,1,128]{2,1,0:T(1,128)}), s32[8,1,128]{2,1,0:T(1,128)}, u32[]{:S(2)}, u32[]{:S(2)}) async-start(s32[8,1,128]{2,1,0:T(1,128)} %reshape.462), calls=%async_computation.3 | async-start | bytes 8192 | tf_op jit(solution)/shard_map/all_to_all | solution.py:638
  38.4 63.4 %copy-start.30 = (s32[1024,1]{0,1:T(1,128)S(1)}, s32[1024,1]{0,1:T(1,128)}, u32[]{:S(2)}) copy-start(s32[1024,1]{0,1:T(1,128)} %copy-done.29) | copy-start | bytes 12292
  97.6 40.6 %all-to-all-start.5 = ((bf16[8,16,8,768]{3,2,1,0:T(8,128)(2,1)}), bf16[8,16,8,768]{3,2,1,0:T(8,128)(2,1)}, u32[]{:S(2)}, u32[]{:S(2)}) async-start(bf16[8,16,8,768]{3,2,1,0:T(8,128)(2,1)} %param.24), calls=%async_computation.5 | async-start | bytes 3145728 | tf_op jit(solution)/shard_map/all_to_all | solution.py:638
  109.4 33.3 %copy-start.40 = (bf16[768]{0:T(1024)(128)(2,1)S(1)}, bf16[768]{0:T(1024)(128)(2,1)}, u32[]{:S(2)}) copy-start(bf16[768]{0:T(1024)(128)(2,1)} %param.39) | copy-start | bytes 4612
  109.4 33.3 %copy-start.38 = (bf16[768]{0:T(1024)(128)(2,1)S(1)}, bf16[768]{0:T(1024)(128)(2,1)}, u32[]{:S(2)}) copy-start(bf16[768]{0:T(1024)(128)(2,1)} %param.30) | copy-start | bytes 4612
  109.4 33.3 %copy-start.39 = (bf16[768]{0:T(1024)(128)(2,1)S(1)}, bf16[768]{0:T(1024)(128)(2,1)}, u32[]{:S(2)}) copy-start(bf16[768]{0:T(1024)(128)(2,1)} %param.32) | copy-start | bytes 4612
  138.2 78.3 %all-to-all-start.2 = ((bf16[8,16,8,768]{3,2,1,0:T(8,128)(2,1)}), bf16[8,16,8,768]{3,2,1,0:T(8,128)(2,1)}, u32[]{:S(2)}, u32[]{:S(2)}) async-start(bf16[8,16,8,768]{3,2,1,0:T(8,128)(2,1)} %bitcast.111), calls=%async_computation.2 | async-start | bytes 3145728 | tf_op jit(solution)/shard_map/all_to_all | solution.py:638
  192.6 20.4 %copy-start.1 = (bf16[9,1024,128]{2,1,0:T(8,128)(2,1)}, bf16[9,1024,128]{2,1,0:T(8,128)(2,1)S(1)}, u32[]{:S(2)}) copy-start(bf16[9,1024,128]{2,1,0:T(8,128)(2,1)S(1)} %broadcast_in_dim.30.mask_ref) | copy-start | bytes 7077892
  228.5 132.7 %copy-start.13 = (f32[2,16,4,8,768]{4,3,2,1,0:T(8,128)}, f32[2,16,4,8,768]{4,3,2,1,0:T(8,128)S(1)}, u32[]{:S(2)}) copy-start(f32[2,16,4,8,768]{4,3,2,1,0:T(8,128)S(1)} %copy.90) | copy-start | bytes 9437188
  235.9 24.6 %copy-start.3 = (bf16[1024,768]{1,0:T(8,128)(2,1)}, bf16[1024,768]{1,0:T(8,128)(2,1)S(1)}, u32[]{:S(2)}) copy-start(bf16[1024,768]{1,0:T(8,128)(2,1)S(1)} %get-tuple-element.45.q_ref) | copy-start | bytes 4718596
  235.9 24.6 %copy-start.37 = (f32[768]{0:T(1024)S(1)}, f32[768]{0:T(1024)}, u32[]{:S(2)}) copy-start(f32[768]{0:T(1024)} %convert_element_type.175) | copy-start | bytes 9220
  236.0 24.6 %copy-start.41 = (bf16[768,768]{1,0:T(8,128)(2,1)S(1)}, bf16[768,768]{1,0:T(8,128)(2,1)}, u32[]{:S(2)}) copy-start(bf16[768,768]{1,0:T(8,128)(2,1)} %param.28) | copy-start | bytes 3538948
  262.2 47.5 %copy-start.18 = (f32[1024,768]{1,0:T(8,128)}, f32[1024,768]{1,0:T(8,128)S(1)}, u32[]{:S(2)}) copy-start(f32[1024,768]{1,0:T(8,128)S(1)} %get-tuple-element.76) | copy-start | bytes 9437188
  265.2 11.8 %copy-start.5 = (bf16[1024,768]{1,0:T(8,128)(2,1)S(1)}, bf16[1024,768]{1,0:T(8,128)(2,1)}, u32[]{:S(2)}) copy-start(bf16[1024,768]{1,0:T(8,128)(2,1)} %copy-done.4) | copy-start | bytes 4718596
  355.5 12.0 %slice-start.2 = ((s8[4718592]{0:T(1024)(128)(4,1)}), s8[4194304]{0:T(1024)(128)(4,1)S(1)}, s32[]{:S(2)}) async-start(s8[4718592]{0:T(1024)(128)(4,1)} %bitcast.138), calls=%async_computation.9 | async-start | bytes 8388608
  355.5 12.0 %slice-start.4 = ((s8[6291456]{0:T(1024)(128)(4,1)}), s8[4194304]{0:T(1024)(128)(4,1)S(1)}, s32[]{:S(2)}) async-start(s8[6291456]{0:T(1024)(128)(4,1)} %bitcast.140), calls=%async_computation.11 | async-start | bytes 8388608
  361.2 6.3 %copy-start.19 = (f32[1024,768]{1,0:T(8,128)S(1)}, f32[1024,768]{1,0:T(8,128)}, u32[]{:S(2)}) copy-start(f32[1024,768]{1,0:T(8,128)} %copy-done.18) | copy-start | bytes 9437188
  361.2 6.3 %copy-start.35 = (f32[768]{0:T(1024)S(1)}, f32[768]{0:T(1024)}, u32[]{:S(2)}) copy-start(f32[768]{0:T(1024)} %convert_element_type.181) | copy-start | bytes 9220
  361.2 6.3 %slice-start.3 = ((s8[4718592]{0:T(1024)(128)(4,1)}), s8[524288]{0:T(1024)(128)(4,1)S(1)}, s32[]{:S(2)}) async-start(s8[4718592]{0:T(1024)(128)(4,1)} %bitcast.138), calls=%async_computation.10 | async-start | bytes 1048576
  361.2 6.3 %slice-start.5 = ((s8[6291456]{0:T(1024)(128)(4,1)}), s8[2097152]{0:T(1024)(128)(4,1)S(1)}, s32[]{:S(2)}) async-start(s8[6291456]{0:T(1024)(128)(4,1)} %bitcast.140), calls=%async_computation.12 | async-start | bytes 4194304
  367.5 5.1 copy-start.2
  372.6 15.7 %copy-start.10 = (bf16[1024,768]{1,0:T(8,128)(2,1)}, bf16[1024,768]{1,0:T(8,128)(2,1)S(1)}, u32[]{:S(2)}) copy-start(bf16[1024,768]{1,0:T(8,128)(2,1)S(1)} %add_convert_fusion.1.rows_ref) | copy-start | bytes 4718596
  388.3 7.5 %copy-start.23 = (f32[1024]{0:T(1024)S(1)}, f32[1024]{0:T(1024)}, u32[]{:S(2)}) copy-start(f32[1024]{0:T(1024)} %add.174) | copy-start | bytes 12292
  389.5 41.5 %all-to-all-start.4 = ((bf16[8,16,8,768]{3,2,1,0:T(8,128)(2,1)}), bf16[8,16,8,768]{3,2,1,0:T(8,128)(2,1)}, u32[]{:S(2)}, u32[]{:S(2)}) async-start(bf16[8,16,8,768]{3,2,1,0:T(8,128)(2,1)} %bitcast.110), calls=%async_computation.4 | async-start | bytes 3145728 | tf_op jit(solution)/shard_map/all_to_all | solution.py:649
  396.5 4.7 copy-start.17
  396.5 4.7 copy-start.25
  431.0 187.6 %all-to-all-start.6 = ((bf16[8,16,8,768]{3,2,1,0:T(8,128)(2,1)}), bf16[8,16,8,768]{3,2,1,0:T(8,128)(2,1)}, u32[]{:S(2)}, u32[]{:S(2)}) async-start(bf16[8,16,8,768]{3,2,1,0:T(8,128)(2,1)} %bitcast.109), calls=%async_computation.6 | async-start | bytes 3145728 | tf_op jit(solution)/shard_map/all_to_all | solution.py:649
  435.6 13.1 %copy-start.33 = (bf16[768]{0:T(1024)(128)(2,1)S(1)}, bf16[768]{0:T(1024)(128)(2,1)}, u32[]{:S(2)}) copy-start(bf16[768]{0:T(1024)(128)(2,1)} %get-tuple-element.33) | copy-start | bytes 4612
  435.6 13.8 %copy-start.34 = (bf16[8,96]{1,0:T(8,128)(2,1)S(1)}, bf16[8,96]{1,0:T(8,128)(2,1)}, u32[]{:S(2)}) copy-start(bf16[8,96]{1,0:T(8,128)(2,1)} %reshape.427) | copy-start | bytes 4612
  (23 other events, 56.5 us)

commit v3 on v2

--- a/solution.py
+++ b/solution.py
@@ -473,14 +473,6 @@
     )
 
 
-def mark_columns(marks):
-    lane = lax.broadcasted_iota(jnp.int32, (1, 128), 1) % 64
-    hot = marks[:, None] == lane
-    query_side = jnp.where(hot, 1.0, 0.0)
-    key_side = jnp.where((lane < 3) & ~hot, -far, 0.0)
-    return query_side.astype(jnp.bfloat16), key_side.astype(jnp.bfloat16)
-
-
 def attend_kernel(q_ref, k_ref, v_ref, qa_ref, ka_ref, o_ref, col_ref):
     lane = lax.broadcasted_iota(jnp.int32, (1, 128), 1)
     low = lane < 64
@@ -605,7 +597,7 @@
     )(queries, key_rows, values, columns, key_marks, out, grad)
 
 
-def fetch_codes(code_ids, embed_table, first):
+def fetch_codes(code_ids, embed_table):
     features = embed_table.shape[1]
     holder_count = lax.axis_size(("ty", "tx"))
     share_rows = embed_table.shape[0]
@@ -626,11 +618,7 @@
     requests = requests.reshape(holder_count, slot_count)
     asked = lax.all_to_all(requests, ("ty", "tx"), split_axis=0, concat_axis=0, tiled=True)
     fetched = embed_table.at[asked.reshape(-1)].get(mode="promise_in_bounds")
-    fetched, _ = lax.optimization_barrier((fetched, first))
-    fetched = fetched.reshape(holder_count, slot_count, features)
-    returned = lax.all_to_all(fetched, ("ty", "tx"), split_axis=0, concat_axis=0, tiled=True)
-    returned = returned.reshape(holder_count * slot_count, features)
-    return returned.at[slot_index].get(mode="promise_in_bounds")
+    return slot_index, fetched.reshape(holder_count, slot_count, features)
 
 
 def to_grid(tiles):
@@ -676,7 +664,9 @@
     for i in range(4):
         rows = slice(i * step, (i + 1) * step)
         first = pl.multiple_of(down * width + i * step, width)
-        mask = jnp.concatenate([mask_ref[0, rows, :]] * (features // 128), axis=1)
+        same = mask_ref[right, pl.ds(first, step), :] == mask_ref[1, width + i * step : width + (i + 1) * step, :]
+        mask = jnp.where(same, 1.0, 0.0).astype(jnp.bfloat16)
+        mask = jnp.concatenate([mask] * (features // 128), axis=1)
         taken = shifted[right, pl.ds(first, step), :] * mask
         if sign < 0:
             taps_ref[rows, :] = taken
@@ -705,13 +695,12 @@
         taps = jax.ShapeDtypeStruct((tokens, 9 * features), jnp.bfloat16)
         out_shape = [jax.ShapeDtypeStruct((tokens, features), jnp.float32), low, taps]
         out_specs = [out_specs, out_specs, pl.BlockSpec((tokens, features), lambda k: (0, k))]
-    tap_of = (lambda k: (k, 0, 0)) if sign > 0 else (lambda k: (8 - k, 0, 0))
     return pl.pallas_call(
         partial(conv_kernel, width=width, sign=sign),
         grid=(9,),
         in_specs=[
             whole((tokens, features)),
-            pl.BlockSpec((1, tokens, 128), tap_of),
+            pl.BlockSpec(masks.shape, lambda k: (0, 0, 0)),
             pl.BlockSpec((1, features, features), lambda k: (k, 0, 0)),
             whole((1, features)),
         ],
@@ -731,30 +720,320 @@
     )(rows, masks, weight, bias)
 
 
-def tap_masks(marks_grid):
-    height, width = marks_grid.shape
-    padded = jnp.pad(marks_grid, ((1, 1), (1, 1)), constant_values=-1)
-    masks = jnp.stack(
-        [
-            (padded[a : a + height, b : b + width] == marks_grid).reshape(height * width)
-            for a in range(3)
-            for b in range(3)
-        ]
-    ).astype(jnp.bfloat16)
-    return jnp.broadcast_to(masks[:, :, None], (9, height * width, 128))
+def marks_kernel(parts_ref, moved_ref, query_ref, key_ref, *, down, across, rows, cols):
+    width = across * cols
+    tokens = down * rows * width
+    turned = parts_ref[...].astype(jnp.float32).T
+    nowhere = jnp.full((width, 128), -1.0, jnp.float32)
+    for j in range(3):
+        moved_ref[j, 0:width, :] = nowhere
+        moved_ref[j, width + tokens :, :] = nowhere
+    for part in range(down * across):
+        spread = jnp.broadcast_to(turned[:, part : part + 1], (rows * cols, 128))
+        for r in range(rows):
+            first = ((part // across) * rows + r) * width + (part % across) * cols + width
+            moved_ref[1, first : first + cols, :] = spread[r * cols : (r + 1) * cols]
+    marks = moved_ref[1, width : width + tokens, :]
+    column = lax.broadcasted_iota(jnp.int32, (tokens, 128), 0) % width
+    left = jnp.where(column == 0, -1.0, pltpu.roll(marks, 1, 0))
+    right = jnp.where(column == width - 1, -1.0, pltpu.roll(marks, tokens - 1, 0))
+    moved_ref[0, width : width + tokens, :] = left
+    moved_ref[2, width : width + tokens, :] = right
+    lane = lax.broadcasted_iota(jnp.int32, (tokens, 128), 1) % 64
+    hot = marks == lane.astype(jnp.float32)
+    query_ref[...] = jnp.where(hot, 1.0, 0.0).astype(jnp.bfloat16)
+    key_ref[...] = jnp.where((lane < 3) & ~hot, -far, 0.0).astype(jnp.bfloat16)
+
+
+def spread_marks(parts, down, across, rows, cols):
+    tokens = down * across * rows * cols
+    low = jax.ShapeDtypeStruct((tokens, 128), jnp.bfloat16)
+    return pl.pallas_call(
+        partial(marks_kernel, down=down, across=across, rows=rows, cols=cols),
+        out_shape=[
+            jax.ShapeDtypeStruct((3, tokens + 2 * across * cols, 128), jnp.float32),
+            low,
+            low,
+        ],
+        compiler_params=pltpu.CompilerParams(vmem_limit_bytes=48 * 2**20),
+        name="spread_marks",
+    )(parts)
+
+
+def normalize(values):
+    center = values - jnp.mean(values, axis=-1, keepdims=True)
+    scale = lax.rsqrt(jnp.mean(center * center, axis=-1, keepdims=True) + epsilon)
+    return center * scale, scale
+
+
+def norm_back(grad, gain, unit, scale):
+    scaled = grad * gain
+    mean = jnp.mean(scaled, axis=-1, keepdims=True)
+    along = jnp.mean(scaled * unit, axis=-1, keepdims=True)
+    return scale * (scaled - mean - unit * along)
+
+
+def row(ref):
+    return ref[...].astype(jnp.float32)
+
+
+def add_rows(ref, values):
+    ref[...] += jnp.sum(values, axis=0, keepdims=True)
+
+
+def enter_kernel(
+    codes_ref, gain_ref, shift_ref, weight_ref, qb_ref, vb_ref, normed_ref, q_ref, k_ref, v_ref
+):
+    features = codes_ref.shape[1]
+    unit, _ = normalize(row(codes_ref))
+    normed = (unit * row(gain_ref) + row(shift_ref)).astype(jnp.bfloat16)
+    normed_ref[...] = normed
+    queries = nn(normed, weight_ref[:, 0:features]) + row(qb_ref)
+    q_ref[...] = queries.astype(jnp.bfloat16) * jnp.asarray(HEAD_DIM**-0.5, jnp.bfloat16)
+    k_ref[...] = nn(normed, weight_ref[:, features : 2 * features]).astype(jnp.bfloat16)
+    values = nn(normed, weight_ref[:, 2 * features :]) + row(vb_ref)
+    v_ref[...] = values.astype(jnp.bfloat16)
+
+
+def held(shape):
+    return pl.BlockSpec(shape, lambda i: (0,) * len(shape), pipeline_mode=pl.Buffered(1))
+
+
+def by_rows(step, columns):
+    return pl.BlockSpec((step, columns), lambda i: (i, 0))
+
+
+def enter(codes, gain, shift, weight, query_bias, value_bias, step=256):
+    tokens, features = codes.shape
+    block = by_rows(step, features)
+    vector = held((1, features))
+    return pl.pallas_call(
+        enter_kernel,
+        grid=(tokens // step,),
+        in_specs=[block, vector, vector, held(weight.shape), vector, vector],
+        out_specs=[block] * 4,
+        out_shape=[jax.ShapeDtypeStruct((tokens, features), jnp.bfloat16)] * 4,
+        compiler_params=pltpu.CompilerParams(vmem_limit_bytes=48 * 2**20),
+        cost_estimate=pl.CostEstimate(
+            flops=6 * tokens * features * features,
+            bytes_accessed=6 * features * features + 10 * tokens * features,
+            transcendentals=0,
+        ),
+        name="enter",
+    )(codes, gain, shift, weight, query_bias, value_bias)
 
 
 def gelu_parts(values):
     spread = jnp.exp(-0.5 * values * values)
-    upto = 0.5 * (1.0 + lax.erf(values * 0.7071067811865476))
+    t = 1.0 / (1.0 + (0.3275911 * 0.5**0.5) * jnp.abs(values))
+    series = 0.5 * 1.061405429
+    for factor in (-1.453152027, 1.421413741, -0.284496736, 0.254829592):
+        series = series * t + 0.5 * factor
+    tail = series * t * spread
+    upto = jnp.where(values < 0.0, tail, 1.0 - tail)
     return values * upto, upto + values * spread * 0.3989422804014327
 
 
-def sum_kernel(*refs, layout, count, lead):
+def middle_kernel(
+    codes_ref,
+    attended_ref,
+    final_ref,
+    hidden_grad_ref,
+    out_weight_ref,
+    up_ref,
+    down_ref,
+    out_bias_ref,
+    gain_ref,
+    shift_ref,
+    up_bias_ref,
+    down_bias_ref,
+    features_ref,
+    normed_ref,
+    hidden_ref,
+    pre_ref,
+    middle_grad_ref,
+    branch_ref,
+    attended_grad_ref,
+    out_bias_sum,
+    gain_sum,
+    shift_sum,
+    up_bias_sum,
+):
+    @pl.when(pl.program_id(0) == 0)
+    def _():
+        for ref in (out_bias_sum, gain_sum, shift_sum, up_bias_sum):
+            ref[...] = jnp.zeros_like(ref)
+
+    features = codes_ref.shape[1]
+    middle = row(codes_ref) + (nn(attended_ref[...], out_weight_ref[...]) + row(out_bias_ref))
+    unit, scale = normalize(middle)
+    normed = (unit * row(gain_ref) + row(shift_ref)).astype(jnp.bfloat16)
+    normed_ref[...] = normed
+    total = middle + row(down_bias_ref)
+    grad = jnp.zeros_like(middle)
+    for first in range(0, up_ref.shape[1], features):
+        columns = slice(first, first + features)
+        weight = up_ref[:, columns]
+        hidden_pre = nn(normed, weight) + up_bias_ref[:, columns].astype(jnp.float32)
+        act, slope = gelu_parts(hidden_pre)
+        hidden = act.astype(jnp.bfloat16)
+        hidden_ref[:, columns] = hidden
+        pre = (hidden_grad_ref[:, columns].astype(jnp.float32) * slope).astype(jnp.bfloat16)
+        pre_ref[:, columns] = pre
+        up_bias_sum[:, columns] += jnp.sum(pre.astype(jnp.float32), axis=0, keepdims=True)
+        total = total + nn(hidden, down_ref[columns, :])
+        grad = grad + nt(pre, weight)
+    features_ref[...] = total.astype(jnp.bfloat16)
+    add_rows(gain_sum, grad * unit)
+    add_rows(shift_sum, grad)
+    middle_grad = final_ref[...] + norm_back(grad, row(gain_ref), unit, scale)
+    middle_grad_ref[...] = middle_grad
+    branch = middle_grad.astype(jnp.bfloat16)
+    branch_ref[...] = branch
+    add_rows(out_bias_sum, branch.astype(jnp.float32))
+    attended_grad_ref[...] = nt(branch, out_weight_ref[...]).astype(jnp.bfloat16)
+
+
+def middle_block(
+    codes,
+    attended,
+    final_grad,
+    hidden_grad,
+    out_weight,
+    up_weight,
+    down_weight,
+    out_bias,
+    gain,
+    shift,
+    up_bias,
+    down_bias,
+    step=256,
+):
+    tokens, features = codes.shape
+    wide = up_weight.shape[1]
+    block = by_rows(step, features)
+    broad = by_rows(step, wide)
+    vector = held((1, features))
+
+    def like(columns, dtype=jnp.bfloat16, rows=tokens):
+        return jax.ShapeDtypeStruct((rows, columns), dtype)
+
+    def total(columns):
+        return pl.BlockSpec((1, columns), lambda i: (0, 0))
+
+    return pl.pallas_call(
+        middle_kernel,
+        grid=(tokens // step,),
+        in_specs=[
+            block,
+            block,
+            block,
+            broad,
+            held(out_weight.shape),
+            held(up_weight.shape),
+            held(down_weight.shape),
+            vector,
+            vector,
+            vector,
+            held((1, wide)),
+            vector,
+        ],
+        out_specs=[block, block, broad, broad, block, block, block]
+        + [total(features)] * 3
+        + [total(wide)],
+        out_shape=[
+            like(features),
+            like(features),
+            like(wide),
+            like(wide),
+            like(features, jnp.float32),
+            like(features),
+            like(features),
+        ]
+        + [like(features, jnp.float32, 1)] * 3
+        + [like(wide, jnp.float32, 1)],
+        compiler_params=pltpu.CompilerParams(vmem_limit_bytes=56 * 2**20),
+        cost_estimate=pl.CostEstimate(
+            flops=2 * tokens * features * (2 * features + 3 * wide),
+            bytes_accessed=4 * features * wide + 6 * tokens * wide + 16 * tokens * features,
+            transcendentals=2 * tokens * wide,
+        ),
+        name="middle",
+    )(
+        codes,
+        attended,
+        final_grad,
+        hidden_grad,
+        out_weight,
+        up_weight,
+        down_weight,
+        out_bias,
+        gain,
+        shift,
+        up_bias,
+        down_bias,
+    )
+
+
+def leave_kernel(
+    codes_ref,
+    middle_grad_ref,
+    dq_ref,
+    dk_ref,
+    dv_ref,
+    weight_ref,
+    gain_ref,
+    share_ref,
+    gain_sum,
+    shift_sum,
+    query_sum,
+    value_sum,
+):
+    @pl.when(pl.program_id(0) == 0)
+    def _():
+        for ref in (gain_sum, shift_sum, query_sum, value_sum):
+            ref[...] = jnp.zeros_like(ref)
+
+    features = codes_ref.shape[1]
+    grad = nt(dq_ref[...], weight_ref[:, 0:features])
+    grad = grad + nt(dk_ref[...], weight_ref[:, features : 2 * features])
+    grad = grad + nt(dv_ref[...], weight_ref[:, 2 * features :])
+    start = row(codes_ref)
+    unit, scale = normalize(start)
+    add_rows(gain_sum, grad * unit)
+    add_rows(shift_sum, grad)
+    add_rows(query_sum, row(dq_ref))
+    add_rows(value_sum, row(dv_ref))
+    start_grad = middle_grad_ref[...] + norm_back(grad, row(gain_ref), unit, scale)
+    share_ref[...] = (start_grad - 2.0 * commit_weight * start).astype(jnp.bfloat16)
+
+
+def leave(codes, middle_grad, dq, dk, dv, weight, gain, step=256):
+    tokens, features = codes.shape
+    block = by_rows(step, features)
+    total = pl.BlockSpec((1, features), lambda i: (0, 0))
+    return pl.pallas_call(
+        leave_kernel,
+        grid=(tokens // step,),
+        in_specs=[block] * 5 + [held(weight.shape), held((1, features))],
+        out_specs=[block] + [total] * 4,
+        out_shape=[jax.ShapeDtypeStruct((tokens, features), jnp.bfloat16)]
+        + [jax.ShapeDtypeStruct((1, features), jnp.float32)] * 4,
+        compiler_params=pltpu.CompilerParams(vmem_limit_bytes=48 * 2**20),
+        cost_estimate=pl.CostEstimate(
+            flops=6 * tokens * features * features,
+            bytes_accessed=6 * features * features + 14 * tokens * features,
+            transcendentals=0,
+        ),
+        name="leave",
+    )(codes, middle_grad, dq, dk, dv, weight, gain)
+
+
+def sum_kernel(*refs, layout, homes, count, lead):
     ins = refs[: max(item[0] for item in layout) + 1]
-    out = refs[len(ins)]
-    (own, got0, got1, got2, got3, got4, whole) = refs[len(ins) + 1 : len(ins) + 8]
-    (own_sem, s0, r0, s1, r1, s2, r2, s3, r3, s4, r4, s5, r5, s6, r6, out_sem) = refs[len(ins) + 8 :]
+    outs = refs[len(ins) : 2 * len(ins)]
+    (own, got0, got1, got2, got3, got4, whole) = refs[2 * len(ins) : 2 * len(ins) + 7]
+    (own_sem, s0, r0, s1, r1, s2, r2, s3, r3, s4, r4, s5, r5, s6, r6, out_sem) = refs[2 * len(ins) + 7 :]
     gr, ty, tx = lax.axis_index("gr"), lax.axis_index("ty"), lax.axis_index("tx")
     x, core, half, par = gr // 2, gr % 2, tx // 2, tx % 2
     mate = (2 * x + 1 - core, ty, tx)
@@ -881,22 +1160,27 @@
         return 0
 
     lax.fori_loop(0, count, finish, 0)
-    done = pltpu.make_async_copy(whole, out, out_sem)
-    done.start()
-    done.wait()
-
-
-def sum_blocks(ins, layout, collective_id):
+    copies = []
+    for block, (home, prefix, column) in enumerate(homes):
+        out = outs[home] if prefix is None else outs[home].at[prefix]
+        target = out.at[:, :, pl.ds(column, 2 * width)]
+        copies.append(pltpu.make_async_copy(whole.at[block], target, out_sem.at[block]))
+        copies[-1].start()
+    for copy in copies:
+        copy.wait()
+
+
+def sum_blocks(ins, layout, homes, shapes, collective_id):
     blocks = len(layout)
     count = blocks // 2
     rows, width = ins[0].shape[-2], 384
     dma = pltpu.SemaphoreType.DMA
     half_block = pltpu.VMEM((blocks, 2, 2, 2, 2, rows, width), jnp.bfloat16)
     return pl.pallas_call(
-        partial(sum_kernel, layout=layout, count=count, lead=(0, 2, 4, 6, 8, 10)),
+        partial(sum_kernel, layout=layout, homes=homes, count=count, lead=(0, 2, 4, 6, 8, 10)),
         in_specs=[pl.BlockSpec(memory_space=pl.ANY)] * len(ins),
-        out_specs=pl.BlockSpec(memory_space=pl.ANY),
-        out_shape=jax.ShapeDtypeStruct((blocks, 2, rows, 2 * width), jnp.bfloat16),
+        out_specs=[pl.BlockSpec(memory_space=pl.ANY)] * len(ins),
+        out_shape=[jax.ShapeDtypeStruct(shape, jnp.bfloat16) for shape in shapes],
         scratch_shapes=[
             half_block,
             half_block,
@@ -909,7 +1193,7 @@
         + [dma((blocks,))] * 3
         + [dma((count, 2))] * 4
         + [dma((count,))] * 8
-        + [dma],
+        + [dma((blocks,))],
         compiler_params=pltpu.CompilerParams(
             collective_id=collective_id, has_side_effects=True, vmem_limit_bytes=56 * 2**20
         ),
@@ -941,79 +1225,89 @@
 ):
     features = encoder_out.shape[-1]
     wide = jnp.float32
-    marks_grid = to_grid(segments)
+    height = encoder_out.shape[1] * lax.axis_size("ty")
+    width = encoder_out.shape[2] * lax.axis_size("tx")
+    tokens = height * width
+    down, across = lax.axis_size("ty"), lax.axis_size("tx")
+    axes = ("ty", "tx")
+
+    def line(vector):
+        return vector.reshape(1, -1)
+
     cotangent_grid = to_grid(recon_grad)
-    height, width = marks_grid.shape
-    tokens = height * width
-    codes_tile = fetch_codes(code_ids, embed_table, cotangent_grid).reshape(encoder_out.shape)
-    start_rows = to_grid(codes_tile).reshape(tokens, features).astype(wide)
-    query_marks, key_marks = mark_columns(marks_grid.reshape(tokens))
-
-    masks = tap_masks(marks_grid)
+    marks = segments.reshape(segments.shape[0], 1, -1)
+    marks = lax.all_to_all(marks, axes, split_axis=0, concat_axis=0, tiled=True)
+    moved, query_marks, key_marks = spread_marks(
+        marks.reshape(down * across, -1), down, across, encoder_out.shape[1], encoder_out.shape[2]
+    )
+    slot_index, fetched = fetch_codes(code_ids, embed_table)
+    fetched, cotangent_grid = lax.optimization_barrier((fetched, cotangent_grid))
+    returned = lax.all_to_all(fetched, axes, split_axis=0, concat_axis=0, tiled=True)
+    returned = returned.reshape(-1, features)
+
     cotangent = cotangent_grid.reshape(tokens, features)
     pixel_taps = jnp.swapaxes(pixel_weight, 0, 1)
     final_grad, lower_grad, behind = conv(
-        cotangent, masks, pixel_taps, pixel_bias.reshape(1, features), width, -1
-    )
+        cotangent, moved, pixel_taps, line(pixel_bias), width, -1
+    )
+    returned, lower_grad = lax.optimization_barrier((returned, lower_grad))
+    codes_tile = returned.at[slot_index].get(mode="promise_in_bounds").reshape(encoder_out.shape)
+    codes = to_grid(codes_tile).reshape(tokens, features)
+    hidden_grad = right_product(lower_grad, down_weight).astype(jnp.bfloat16)
     pixel_bias_grad = jnp.sum(cotangent.astype(wide), axis=0)
     down_bias_grad = jnp.sum(lower_grad.astype(wide), axis=0)
-    hidden_grad = right_product(lower_grad, down_weight)
-
-    normed, first_pull = jax.vjp(
-        layer_norm, start_rows, first_gain.astype(wide), first_shift.astype(wide)
-    )
-    normed_low = normed.astype(jnp.bfloat16)
-    projected = matmul(normed_low, qkv_weight)
-    scale = HEAD_DIM**-0.5
-    queries = (projected[:, :features] + query_bias.astype(wide)).astype(jnp.bfloat16)
-    queries = queries * jnp.asarray(scale, jnp.bfloat16)
-    key_rows = projected[:, features : 2 * features].astype(jnp.bfloat16)
-    values = (projected[:, 2 * features :] + value_bias.astype(wide)).astype(jnp.bfloat16)
+
+    normed, queries, key_rows, values = enter(
+        codes, line(first_gain), line(first_shift), qkv_weight, line(query_bias), line(value_bias)
+    )
     attended, columns = attend(queries, key_rows, values, query_marks, key_marks)
-    middle = start_rows + (matmul(attended, out_weight) + out_bias.astype(wide))
-    normed_two, second_pull = jax.vjp(
-        layer_norm, middle, second_gain.astype(wide), second_shift.astype(wide)
-    )
-    normed_two_low = normed_two.astype(jnp.bfloat16)
-    hidden_pre = matmul(normed_two_low, up_weight) + up_bias.astype(wide)
-    hidden_act, slope = gelu_parts(hidden_pre)
-    hidden_low = hidden_act.astype(jnp.bfloat16)
-    pre_grad = (hidden_grad * slope).astype(jnp.bfloat16)
-    output_rows = middle + (matmul(hidden_low, down_weight) + down_bias.astype(wide))
-    features_low = output_rows.astype(jnp.bfloat16)
-
-    recon_rows = conv(features_low, masks, pixel_taps, pixel_bias.reshape(1, features), width, 1)
+    (
+        features_low,
+        normed_two,
+        hidden_low,
+        pre_grad,
+        middle_grad,
+        branch_grad,
+        attended_grad,
+        out_bias_grad,
+        second_gain_grad,
+        second_shift_grad,
+        up_bias_grad,
+    ) = middle_block(
+        codes,
+        attended,
+        final_grad,
+        hidden_grad,
+        out_weight,
+        up_weight,
+        down_weight,
+        line(out_bias),
+        line(second_gain),
+        line(second_shift),
+        line(up_bias),
+        line(down_bias),
+    )
+
+    recon_rows = conv(features_low, moved, pixel_taps, line(pixel_bias), width, 1)
     recon_tiles = to_tiles(recon_rows.reshape(height, width, features))
 
-    pixel_weight_grad = left_product(features_low, behind)
-    down_weight_grad = left_product(hidden_low, lower_grad)
-    up_weight_grad = left_product(normed_two_low, pre_grad)
-    up_bias_grad = jnp.sum(pre_grad.astype(wide), axis=0)
-
-    middle_part, second_gain_grad, second_shift_grad = second_pull(
-        right_product(pre_grad, up_weight)
-    )
-    middle_grad = final_grad + middle_part
-    branch_grad = middle_grad.astype(jnp.bfloat16)
-    out_weight_grad = left_product(attended, branch_grad)
-    out_bias_grad = jnp.sum(branch_grad.astype(wide), axis=0)
-    attended_grad = right_product(branch_grad, out_weight).astype(jnp.bfloat16)
     query_grad, key_grad, value_grad = attend_back_grid(
         queries, key_rows, values, columns, key_marks, attended, attended_grad
     )
-    projected_grad = jnp.concatenate([query_grad, key_grad, value_grad], axis=1)
-    qkv_weight_grad = left_product(normed_low, projected_grad)
-    query_bias_grad = jnp.sum(query_grad.astype(wide), axis=0)
-    value_bias_grad = jnp.sum(value_grad.astype(wide), axis=0)
-    start_part, first_gain_grad, first_shift_grad = first_pull(
-        right_product(projected_grad, qkv_weight)
-    )
-    start_grad = middle_grad + start_part
-    share = (start_grad - 2.0 * commit_weight * start_rows).astype(jnp.bfloat16)
+    share, first_gain_grad, first_shift_grad, query_bias_grad, value_bias_grad = leave(
+        codes, middle_grad, query_grad, key_grad, value_grad, qkv_weight, line(first_gain)
+    )
     share_tiles = to_tiles(share.reshape(height, width, features))
     input_tiles = (
         share_tiles.astype(wide) + 2.0 * commit_weight * encoder_out.astype(wide)
     ).astype(jnp.bfloat16)
+
+    pixel_weight_grad = left_product(features_low, behind)
+    down_weight_grad = left_product(hidden_low, lower_grad)
+    up_weight_grad = left_product(normed_two, pre_grad)
+    out_weight_grad = left_product(attended, branch_grad)
+    projected_grad = jnp.concatenate([query_grad, key_grad, value_grad], axis=1)
+    qkv_weight_grad = left_product(normed, projected_grad)
 
     vectors = [
         query_bias_grad,
@@ -1027,7 +1321,7 @@
         down_bias_grad,
         pixel_bias_grad,
     ]
-    shards = lax.axis_size(("ty", "tx"))
+    shards = down * across
     rows = features // shards
     packed = jnp.concatenate([v.reshape(shards, -1) for v in vectors], axis=1)
     packed = jnp.pad(packed, ((0, 0), (0, rows * features - packed.shape[1])))
@@ -1051,12 +1345,17 @@
     layout += [(3, None, 0)]
     layout += [(4, None, features * k) for k in range(3)]
     layout += [(5, None, 0)]
-    summed = sum_blocks(ins, layout, 1).reshape(len(layout), rows, features).astype(wide)
-    packed = summed[21].reshape(-1)
+    homes = [(0, k, 0) for k in range(9)] + layout[9:]
+    shapes = [(9, 2, rows // 2, features)] + [grad.shape[3:] for grad in ins[1:]]
+    pixel_sum, up_sum, down_sum, out_sum, qkv_sum, packed = [
+        summed.reshape(-1, summed.shape[-1]).astype(wide)
+        for summed in sum_blocks(ins, layout, homes, shapes, 1)
+    ]
+    packed = packed[:8].reshape(-1)
     sums = []
     at = 0
     for vector in vectors:
-        size = vector.shape[0] // shards
+        size = vector.size // shards
         sums.append(packed[at : at + size])
         at += size
     (query_bias_sum, value_bias_sum, out_bias_sum, first_gain_sum, first_shift_sum) = sums[:5]
@@ -1064,20 +1363,20 @@
     return (
         recon_tiles,
         input_tiles,
-        jnp.swapaxes(summed[18:21], 0, 1).reshape(rows, 3 * features),
+        qkv_sum,
         query_bias_sum,
         value_bias_sum,
-        summed[17],
+        out_sum,
         out_bias_sum,
         first_gain_sum,
         first_shift_sum,
         second_gain_sum,
         second_shift_sum,
-        jnp.swapaxes(summed[9:13], 0, 1).reshape(rows, 4 * features),
+        up_sum,
         up_bias_sum,
-        summed[13:17].reshape(4 * rows, features),
+        down_sum,
         down_bias_sum,
-        jnp.swapaxes(summed[0:9], 0, 1),
+        jnp.swapaxes(pixel_sum.reshape(9, rows, features), 0, 1),
         pixel_bias_sum,
     )
 

time: 633 us -> 554 us (0.88)
  Pallas kernels: 237 us -> 297 us
  local copies, waits for them, and re-layouts: 107 us -> 47.8 us
  waiting for transfers between devices: 39.5 us -> 89.7 us
  matrix products: 102 us -> 56.3 us
  blocking collectives: 59.1 us -> 13.6 us
  other arithmetic: 48.1 us -> 12.5 us
    pallas_call x1 -> x5, Pallas kernels: 139 us -> 201 us  [the longest x1 147 us: sum_blocks(): pl.pallas_call(partial(sum_kernel, layout=layout, homes=homes, count=coun...]
    all_to_all x1, blocking collectives: 59.1 us -> 13.6 us  [fetch_codes(): lax.all_to_all(requests, ('ty', 'tx'), split_axis=0, concat_axis=0, tiled...]
    all_to_all x3 -> x2, waiting for transfers between devices: 28.8 us -> 58.3 us  [to_grid(): lax.all_to_all(tiles, ('ty', 'tx'), split_axis=0, concat_axis=0, tiled=True)]
    all_to_all x1 -> x2, waiting for transfers between devices: 5.09 us -> 31.3 us  [the longest x1 31.3 us: on_device_grids(): lax.all_to_all(fetched, axes, split_axis=0, concat_axis=0, tiled=True)]
    dot_general x5 -> x1, matrix products: 22.7 us -> 0.47 us  [matmul(): return jnp.dot(left_side, right_side, preferred_element_type=jnp.float32)]
    dot_general x4 -> x1, matrix products: 31.5 us -> 9.26 us  [right_product(): lax.dot_general(left_side, right_side, (((1,), (1,)), ((), ())), preferre...]
    another operation x11 -> x0, local copies, waits for them, and re-layouts: 14 us -> none  [the longest x10 12.3 us: tap_masks(): jnp.stack([(padded[a:a + height, b:b + width] == marks_grid).reshape(heig...]
    convert_element_type x15 -> x4, other arithmetic: 19.9 us -> 5.95 us  [on_device_grids(): summed.reshape(-1, summed.shape[-1]).astype(wide)]
  transfers between devices with their start and end apart: 6 -> 6, of which waited for: 3 -> 3; matrix products, arithmetic and copies ran while one was open for 23% -> 14% of each run, Pallas kernels for 25% -> 30%
where the time goes in v3:
time: 554 us; the launch traced here: 546 us
  Pallas kernels  297 us (54%)
  waiting for transfers between devices  89.7 us (16%)
  matrix products  56.3 us (10%)
  local copies, waits for them, and re-layouts  47.8 us (9%)
  starting transfers between devices  27.7 us (5%)
  blocking collectives  13.6 us (2%)
  other arithmetic  12.5 us (2%)
    pallas_call x1, Pallas kernels, sum_blocks(): pl.pallas_call(partial(sum_kernel, layout=layout, homes=homes, count=coun...  147 us
    all_to_all x2, waiting for transfers between devices, to_grid(): lax.all_to_all(tiles, ('ty', 'tx'), split_axis=0, concat_axis=0, tiled=True)  58.3 us
    dot_general x5, matrix products, left_product(): lax.dot_general(left_side, right_side, (((0,), (0,)), ((), ())), preferre...  46.6 us
    pallas_call x1, Pallas kernels, attend_back_grid(): pl.pallas_call(partial(attend_back_kernel, step=min(512, tokens)), grid=(...  37.6 us
    pallas_call x1, Pallas kernels, middle_block(): pl.pallas_call(middle_kernel, grid=(tokens // step,), in_specs=[block, bl...  36.7 us
    pallas_call x2, Pallas kernels, conv(): pl.pallas_call(partial(conv_kernel, width=width, sign=sign), grid=(9,), i...  34.5 us
    all_to_all x1, waiting for transfers between devices, on_device_grids(): lax.all_to_all(fetched, axes, split_axis=0, concat_axis=0, tiled=True)  31.3 us
    pallas_call x1, Pallas kernels, attend(): pl.pallas_call(attend_kernel, grid=(features // 128,), in_specs=[pair, pa...  24.1 us
  transfers between devices with their start and end apart: 6, of which 3 were waited for; matrix products, arithmetic and copies ran while one was open for 14% of the time, Pallas kernels for 30%

profile of v3, /device:TPU:0, one launch (start us, length us, event | category | flops | bytes accessed | tf_op | source)
XLA Modules:
  0.0 546.2 jit_solution(2027290223105477825)
XLA Ops:
  2.2 4.3 scatter_custom_fusion
  6.6 13.6 %all_to_all.39 = s32[8,1,192]{2,1,0:T(1,128)S(1)} all-to-all(s32[8,1,192]{2,1,0:T(1,128)S(1)} %all_to_all.24), channel_id=1, replica_groups=mesh['gr'=4,'ty'=2,'tx'=4] {'ty','tx'}, dimensions={0} | all-to-all | bytes 12288 | tf_op jit(solution)/shard_map/all_to_all | solution.py:619
  20.2 3.7 all-to-all-start.1
  24.8 35.7 %all-to-all-done.1 = bf16[8,16,8,768]{3,2,1,0:T(8,128)(2,1)S(1)} async-done(((bf16[8,16,8,768]{3,2,1,0:T(8,128)(2,1)}), bf16[8,16,8,768]{3,2,1,0:T(8,128)(2,1)S(1)}, u32[]{:S(2)}, u32[]{:S(2)}) %all-to-all-start.1) | async-done | bytes 1572896 | tf_op jit(solution)/shard_map/all_to_all | solution.py:626
  60.6 3.3 all-to-all-start.3
  63.9 11.7 %gather_fusion = bf16[1536,768]{1,0:T(8,128)(2,1)} fusion(bf16[6284,768]{1,0:T(8,128)(2,1)} %param.23, s32[2048]{0:T(1024)S(1)} %pad_clamp_fusion), kind=kCustom, calls=%fused_computation | custom fusion | bytes 4724736 | tf_op jit(solution)/shard_map/gather | solution.py:620
  75.8 5.9 %all-to-all-start.2 = ((bf16[8,192,768]{2,1,0:T(8,128)(2,1)}), bf16[8,192,768]{2,1,0:T(8,128)(2,1)}, u32[]{:S(2)}, u32[]{:S(2)}) async-start(bf16[8,192,768]{2,1,0:T(8,128)(2,1)} %bitcast.72), calls=%async_computation.2 | async-start | bytes 4718592 | tf_op jit(solution)/shard_map/all_to_all | solution.py:1245
  82.8 19.5 %conv.2 = (f32[1024,768]{1,0:T(8,128)}, bf16[1024,768]{1,0:T(8,128)(2,1)S(1)}, bf16[1024,6912]{1,0:T(8,128)(2,1)}) custom-call(bf16[1024,768]{1,0:T(8,128)(2,1)S(1)} %bitcast.63, f32[3,1088,128]{2,1,0:T(8,128)S(1)} %get-tuple-element.60.mask_ref, bf16[9,768,768]{2,1,0:T(8,128)(2,1)} %bitcast.86, bf16[1,768]{1,0:T(2,128)(2,1)S(1)} %reshape.266.bias_ref), custom_call_target="tpu_custom_call" | custom-call | flops 10871635968 | bytes 13762560 | tf_op jit(solution)/shard_map/conv/pallas_call | solution.py:698
  103.5 31.3 %all-to-all-done.2 = bf16[8,192,768]{2,1,0:T(8,128)(2,1)} async-done(((bf16[8,192,768]{2,1,0:T(8,128)(2,1)}), bf16[8,192,768]{2,1,0:T(8,128)(2,1)}, u32[]{:S(2)}, u32[]{:S(2)}) %all-to-all-start.2) | async-done | bytes 2359328 | tf_op jit(solution)/shard_map/all_to_all | solution.py:1245
  134.8 7.5 %gather_fusion.1 = bf16[1024,768]{1,0:T(8,128)(2,1)} fusion(bf16[1536,768]{1,0:T(8,128)(2,1)} %bitcast.6, s32[1024]{0:T(1024)S(1)} %broadcast_clamp_fusion), kind=kCustom, calls=%fused_computation.1 | custom fusion | bytes 3149824 | tf_op jit(solution)/shard_map/gather | solution.py:1254
  142.4 4.6 all-to-all-start.4
  151.0 9.3 %convolution_convert_fusion.1.hidden_grad_ref = bf16[1024,3072]{1,0:T(8,128)(2,1)} fusion(bf16[1024,768]{1,0:T(8,128)(2,1)S(1)} %get-tuple-element.70, bf16[3072,768]{1,0:T(8,128)(2,1)} %down_ref.1), kind=kOutput, calls=%fused_computation.4 | convolution fusion | flops 4834983936 | bytes 12582912 | tf_op jit(solution)/shard_map/dot_general | solution.py:52
  160.2 22.6 %all-to-all-done.4 = bf16[8,16,8,768]{3,2,1,0:T(8,128)(2,1)} async-done(((bf16[8,16,8,768]{3,2,1,0:T(8,128)(2,1)}), bf16[8,16,8,768]{3,2,1,0:T(8,128)(2,1)}, u32[]{:S(2)}, u32[]{:S(2)}) %all-to-all-start.4) | async-done | bytes 1572896 | tf_op jit(solution)/shard_map/all_to_all | solution.py:626
  182.8 2.7 copy.58
  185.6 8.2 %enter.1 = (bf16[1024,768]{1,0:T(8,128)(2,1)S(1)}, bf16[1024,768]{1,0:T(8,128)(2,1)S(1)}, bf16[1024,768]{1,0:T(8,128)(2,1)S(1)}, bf16[1024,768]{1,0:T(8,128)(2,1)}) custom-call(bf16[1024,768]{1,0:T(8,128)(2,1)} %bitcast.65, bf16[1,768]{1,0:T(2,128)(2,1)S(1)} %reshape.269.gain_ref, bf16[1,768]{1,0:T(2,128)(2,1)S(1)} %reshape.270.shift_ref, ...), custom_call_target="tpu_custom_call" | custom-call | flops 3623878656 | bytes 11403264 | tf_op jit(solution)/shard_map/enter/pallas_call | solution.py:810
  194.9 24.1 %attend.1 = (bf16[1024,768]{1,0:T(8,128)(2,1)S(1)}, bf16[1024,768]{1,0:T(8,128)(2,1)S(1)}) custom-call(bf16[1024,768]{1,0:T(8,128)(2,1)S(1)} %get-tuple-element.63.q_ref, bf16[1024,768]{1,0:T(8,128)(2,1)} %copy-done.12, bf16[1024,768]{1,0:T(8,128)(2,1)} %get-tuple-element.65.v_ref, bf16[1024,128]{1,0:T(8,128)(2,1)S(1)} %copy-done.4, ...), custom_call_target="tpu_custom_call" | custom-call | flops 12884901888 | bytes 7864320 | tf_op jit(solution)/shard_map/attend/pallas_call | solution.py:511
  221.5 36.7 %middle.1 = (bf16[1024,768]{1,0:T(8,128)(2,1)}, bf16[1024,768]{1,0:T(8,128)(2,1)}, bf16[1024,3072]{1,0:T(8,128)(2,1)}, bf16[1024,3072]{1,0:T(8,128)(2,1)}, f32[1...) custom-call(bf16[1024,768]{1,0:T(8,128)(2,1)} %bitcast.66, ...), custom_call_target="tpu_custom_call" | custom-call | flops 16911433728 | bytes 40894464 | tf_op jit(solution)/shard_map/middle/pallas_call | solution.py:924
  259.6 15.0 %conv.3 = bf16[1024,768]{1,0:T(8,128)(2,1)S(1)} custom-call(bf16[1024,768]{1,0:T(8,128)(2,1)S(1)} %copy-done.13, f32[3,1088,128]{2,1,0:T(8,128)S(1)} %copy-done.2, bf16[9,768,768]{2,1,0:T(8,128)(2,1)} %bitcast.87, bf16[1,768]{1,0:T(2,128)(2,1)S(1)} %reshape.266.bias_ref), custom_call_target="tpu_custom_call" | custom-call | flops 10871635968 | bytes 13762560 | tf_op jit(solution)/shard_map/conv/pallas_call | solution.py:698
  275.9 37.6 %attend_back.1 = (bf16[1024,768]{1,0:T(8,128)(2,1)S(1)}, bf16[1024,768]{1,0:T(8,128)(2,1)S(1)}, bf16[1024,768]{1,0:T(8,128)(2,1)S(1)}) custom-call(bf16[1024,768]{1,0:T(8,128)(2,1)} %copy-done.11, bf16[1024,768]{1,0:T(8,128)(2,1)} %copy-done.12, bf16[1024,768]{1,0:T(8,128)(2,1)} %get-tuple-element.65.v_ref, bf16[1024,768]{1,0:T(8,128)(2,1)} %copy-done.15, ...), custom_call_target="tpu_custom_call" | custom-call | flops 19327352832 | bytes 14155776 | tf_op jit(solution)/shard_map/attend_back/pallas_call | solution.py:583
  315.8 9.1 %leave.1 = (bf16[1024,768]{1,0:T(8,128)(2,1)S(1)}, f32[1,768]{1,0:T(1,128)S(1)}, f32[1,768]{1,0:T(1,128)S(1)}, f32[1,768]{1,0:T(1,128)S(1)}, f32[1,768]{1,0:T(1,128)S(1)}) custom-call(bf16[1024,768]{1,0:T(8,128)(2,1)S(1)} %bitcast.67, f32[1024,768]{1,0:T(8,128)} %get-tuple-element.72.middle_grad_ref, bf16[1024,768]{1,0:T(8,128)(2,1)S(1)} %get-tuple-element.75.dq_ref, ...), custom_call_target="tpu_custom_call" | custom-call | flops 3623878656 | bytes 14548992 | tf_op jit(solution)/shard_map/leave/pallas_call | solution.py:1015
  324.9 6.1 %convolution_convert_fusion.4 = bf16[768,2304]{1,0:T(8,128)(2,1)} fusion(bf16[1024,768]{1,0:T(8,128)(2,1)S(1)} %get-tuple-element.84, bf16[1024,768]{1,0:T(8,128)(2,1)S(1)} %copy-done.8, bf16[1024,768]{1,0:T(8,128)(2,1)S(1)} %copy-done.6, bf16[1024,768]{1,0:T(8,128)(2,1)S(1)} %get-tuple-element.75.dq_ref), kind=kOutput, calls=%fused_computation.7 | convolution fusion | flops 3639803904 | bytes 9830400 | tf_op jit(solution)/shard_map/dot_general | solution.py:46
  332.3 3.8 all-to-all-start.5
  336.1 9.8 %convolution_convert_fusion.2 = bf16[3072,768]{1,0:T(8,128)(2,1)} fusion(bf16[1024,3072]{1,0:T(8,128)(2,1)} %get-tuple-element.82, bf16[1024,768]{1,0:T(8,128)(2,1)S(1)} %get-tuple-element.70), kind=kOutput, calls=%fused_computation.5 | convolution fusion | flops 4834197504 | bytes 12582912 | tf_op jit(solution)/shard_map/dot_general | solution.py:46
  346.1 9.7 %convolution_convert_fusion.3 = bf16[768,3072]{1,0:T(8,128)(2,1)} fusion(bf16[1024,768]{1,0:T(8,128)(2,1)S(1)} %copy-done.35, bf16[1024,3072]{1,0:T(8,128)(2,1)} %get-tuple-element.81), kind=kOutput, calls=%fused_computation.6 | convolution fusion | flops 4834197504 | bytes 12582912 | tf_op jit(solution)/shard_map/dot_general | solution.py:46
  355.8 2.5 convolution_convert_fusion.5
  358.3 18.5 %convolution_convert_fusion = bf16[768,6912]{1,0:T(8,128)(2,1)} fusion(bf16[1024,768]{1,0:T(8,128)(2,1)S(1)} %copy-done.14, bf16[1024,6912]{1,0:T(8,128)(2,1)} %get-tuple-element.79), kind=kOutput, calls=%fused_computation.3 | convolution fusion | flops 10876944384 | bytes 26345472 | tf_op jit(solution)/shard_map/dot_general | solution.py:46
  376.8 6.3 %all-to-all-start.6 = ((bf16[8,16,8,768]{3,2,1,0:T(8,128)(2,1)}), bf16[8,16,8,768]{3,2,1,0:T(8,128)(2,1)S(1)}, u32[]{:S(2)}, u32[]{:S(2)}) async-start(bf16[8,16,8,768]{3,2,1,0:T(8,128)(2,1)} %bitcast.20), calls=%async_computation.6 | async-start | bytes 3145728 | tf_op jit(solution)/shard_map/all_to_all | solution.py:637
  385.2 146.6 %sum_blocks.1 = (bf16[9,2,48,768]{3,2,1,0:T(8,128)(2,1)}, bf16[2,48,3072]{2,1,0:T(8,128)(2,1)}, bf16[4,2,48,768]{3,2,1,0:T(8,128)(2,1)}, bf16[2,48,768]{2,1,0:T(...) custom-call(bf16[2,2,2,2,48,6912]{5,4,3,2,1,0:T(8,128)(2,1)} %bitcast.71, ...), custom_call_target="tpu_custom_call" | custom-call | tf_op jit(solution)/shard_map/sum_blocks/pallas_call | solution.py:1179
  533.8 1.6 bitcast_convert_fusion.3
  535.4 2.2 bitcast_convert_fusion
  537.6 1.8 convert_bitcast_fusion
  541.8 3.0 add_convert_fusion
  (131 shorter events, 26.2 us)
Async XLA Ops:
  20.2 3.7 copy-start.19
  20.2 40.4 %all-to-all-start.1 = ((bf16[8,16,8,768]{3,2,1,0:T(8,128)(2,1)}), bf16[8,16,8,768]{3,2,1,0:T(8,128)(2,1)S(1)}, u32[]{:S(2)}, u32[]{:S(2)}) async-start(bf16[8,16,8,768]{3,2,1,0:T(8,128)(2,1)} %param.24), calls=%async_computation.1 | async-start | bytes 3145728 | tf_op jit(solution)/shard_map/all_to_all | solution.py:626
  60.6 15.2 %all-to-all-start.3 = ((s32[8,1,128]{2,1,0:T(1,128)}), s32[8,1,128]{2,1,0:T(1,128)S(1)}, u32[]{:S(2)}, u32[]{:S(2)}) async-start(s32[8,1,128]{2,1,0:T(1,128)} %bitcast.8), calls=%async_computation.3 | async-start | bytes 8192 | tf_op jit(solution)/shard_map/all_to_all | solution.py:1239
  75.8 6.0 %copy-start.25 = (bf16[768]{0:T(1024)(128)(2,1)S(1)}, bf16[768]{0:T(1024)(128)(2,1)}, u32[]{:S(2)}) copy-start(bf16[768]{0:T(1024)(128)(2,1)} %param.39) | copy-start | bytes 4612
  75.8 59.0 %all-to-all-start.2 = ((bf16[8,192,768]{2,1,0:T(8,128)(2,1)}), bf16[8,192,768]{2,1,0:T(8,128)(2,1)}, u32[]{:S(2)}, u32[]{:S(2)}) async-start(bf16[8,192,768]{2,1,0:T(8,128)(2,1)} %bitcast.72), calls=%async_computation.2 | async-start | bytes 4718592 | tf_op jit(solution)/shard_map/all_to_all | solution.py:1245
  142.4 4.7 copy-start.26
  142.4 4.7 copy-start.27
  142.4 4.8 copy-start.28
  142.4 4.8 copy-start.29
  142.4 5.4 copy-start.30
  142.4 5.4 copy-start.31
  142.4 5.9 %copy-start.32 = (bf16[768]{0:T(1024)(128)(2,1)S(1)}, bf16[768]{0:T(1024)(128)(2,1)}, u32[]{:S(2)}) copy-start(bf16[768]{0:T(1024)(128)(2,1)} %param.33) | copy-start | bytes 4612
  142.4 6.5 %copy-start.33 = (bf16[768]{0:T(1024)(128)(2,1)S(1)}, bf16[768]{0:T(1024)(128)(2,1)}, u32[]{:S(2)}) copy-start(bf16[768]{0:T(1024)(128)(2,1)} %param.37) | copy-start | bytes 4612
  142.4 7.1 %copy-start.21 = (bf16[3072]{0:T(1024)(128)(2,1)S(1)}, bf16[3072]{0:T(1024)(128)(2,1)}, u32[]{:S(2)}) copy-start(bf16[3072]{0:T(1024)(128)(2,1)} %param.35) | copy-start | bytes 18436
  142.4 40.4 %all-to-all-start.4 = ((bf16[8,16,8,768]{3,2,1,0:T(8,128)(2,1)}), bf16[8,16,8,768]{3,2,1,0:T(8,128)(2,1)}, u32[]{:S(2)}, u32[]{:S(2)}) async-start(bf16[8,16,8,768]{3,2,1,0:T(8,128)(2,1)} %bitcast.75), calls=%async_computation.4 | async-start | bytes 3145728 | tf_op jit(solution)/shard_map/all_to_all | solution.py:626
  185.6 9.4 %copy-start.4 = (bf16[1024,128]{1,0:T(8,128)(2,1)S(1)}, bf16[1024,128]{1,0:T(8,128)(2,1)}, u32[]{:S(2)}) copy-start(bf16[1024,128]{1,0:T(8,128)(2,1)} %copy-done.3) | copy-start | bytes 786436
  194.9 24.1 %copy-start.11 = (bf16[1024,768]{1,0:T(8,128)(2,1)}, bf16[1024,768]{1,0:T(8,128)(2,1)S(1)}, u32[]{:S(2)}) copy-start(bf16[1024,768]{1,0:T(8,128)(2,1)S(1)} %get-tuple-element.63.q_ref) | copy-start | bytes 4718596
  221.5 36.7 %copy-start.2 = (f32[3,1088,128]{2,1,0:T(8,128)S(1)}, f32[3,1088,128]{2,1,0:T(8,128)}, u32[]{:S(2)}) copy-start(f32[3,1088,128]{2,1,0:T(8,128)} %copy-done.1) | copy-start | bytes 5013508
  275.9 39.9 %copy-start = (bf16[2,16,4,8,768]{4,3,2,1,0:T(8,128)(2,1)S(1)}, bf16[2,16,4,8,768]{4,3,2,1,0:T(8,128)(2,1)}, u32[]{:S(2)}) copy-start(bf16[2,16,4,8,768]{4,3,2,1,0:T(8,128)(2,1)} %copy.58) | copy-start | bytes 4718596
  315.8 9.1 %copy-start.6 = (bf16[1024,768]{1,0:T(8,128)(2,1)S(1)}, bf16[1024,768]{1,0:T(8,128)(2,1)}, u32[]{:S(2)}) copy-start(bf16[1024,768]{1,0:T(8,128)(2,1)} %copy-done.5) | copy-start | bytes 4718596
  315.8 9.1 %copy-start.8 = (bf16[1024,768]{1,0:T(8,128)(2,1)S(1)}, bf16[1024,768]{1,0:T(8,128)(2,1)}, u32[]{:S(2)}) copy-start(bf16[1024,768]{1,0:T(8,128)(2,1)} %copy-done.7) | copy-start | bytes 4718596
  332.3 44.5 %all-to-all-start.5 = ((bf16[8,16,8,768]{3,2,1,0:T(8,128)(2,1)}), bf16[8,16,8,768]{3,2,1,0:T(8,128)(2,1)S(1)}, u32[]{:S(2)}, u32[]{:S(2)}) async-start(bf16[8,16,8,768]{3,2,1,0:T(8,128)(2,1)} %bitcast.73), calls=%async_computation.5 | async-start | bytes 3145728 | tf_op jit(solution)/shard_map/all_to_all | solution.py:637
  336.1 9.9 %copy-start.23 = (f32[1,768]{1,0:T(1,128)S(1)}, f32[1,768]{1,0:T(1,128)}, u32[]{:S(2)}) copy-start(f32[1,768]{1,0:T(1,128)} %get-tuple-element.90) | copy-start | bytes 9220
  336.1 9.9 %copy-start.24 = (f32[1,768]{1,0:T(1,128)S(1)}, f32[1,768]{1,0:T(1,128)}, u32[]{:S(2)}) copy-start(f32[1,768]{1,0:T(1,128)} %get-tuple-element.91) | copy-start | bytes 9220
  336.1 10.0 %copy-start.35 = (bf16[1024,768]{1,0:T(8,128)(2,1)S(1)}, bf16[1024,768]{1,0:T(8,128)(2,1)}, u32[]{:S(2)}) copy-start(bf16[1024,768]{1,0:T(8,128)(2,1)} %get-tuple-element.80) | copy-start | bytes 4718596
  346.1 9.7 %copy-start.10 = (bf16[1024,768]{1,0:T(8,128)(2,1)S(1)}, bf16[1024,768]{1,0:T(8,128)(2,1)}, u32[]{:S(2)}) copy-start(bf16[1024,768]{1,0:T(8,128)(2,1)} %copy-done.9) | copy-start | bytes 4718596
  346.1 9.7 %copy-start.34 = (bf16[1024,768]{1,0:T(8,128)(2,1)S(1)}, bf16[1024,768]{1,0:T(8,128)(2,1)}, u32[]{:S(2)}) copy-start(bf16[1024,768]{1,0:T(8,128)(2,1)} %get-tuple-element.83) | copy-start | bytes 4718596
  355.8 2.5 copy-start.14
  376.8 6.4 %copy-start.22 = (f32[1,768]{1,0:T(1,128)S(1)}, f32[1,768]{1,0:T(1,128)}, u32[]{:S(2)}) copy-start(f32[1,768]{1,0:T(1,128)} %get-tuple-element.87) | copy-start | bytes 9220
  376.8 165.0 %all-to-all-start.6 = ((bf16[8,16,8,768]{3,2,1,0:T(8,128)(2,1)}), bf16[8,16,8,768]{3,2,1,0:T(8,128)(2,1)S(1)}, u32[]{:S(2)}, u32[]{:S(2)}) async-start(bf16[8,16,8,768]{3,2,1,0:T(8,128)(2,1)} %bitcast.20), calls=%async_computation.6 | async-start | bytes 3145728 | tf_op jit(solution)/shard_map/all_to_all | solution.py:637
  532.5 5.1 copy-start.16
  537.6 1.8 copy-start.18
  (10 other events, 11.6 us)
